TPU v7x, 512 devices: a whole 4x8x8 slice. The times are simulated.
512 devices in a mesh: gx: 32 (over z, y_hi, core), gy: 16 (over y_lo, x).
Axes of the slice: x: 4, y: 8 (y_hi: 2, y_lo: 4; y = y_hi * 4 + y_lo), z: 8, core: 2. Of those that a mesh axis runs over, the one named last changes fastest.
Arguments:
- forward_state: float32 [9, 256, 256, 128], P(None, 'gx', 'gy'), may hold values from -6 to 6
- adjoint_state: float32 [9, 256, 256, 128], P(None, 'gx', 'gy'), may hold values from -6 to 6
- lame_lambda: float32 [256, 256, 128], P('gx', 'gy'), may hold values from 0.5 to 1.5
- lame_mu: float32 [256, 256, 128], P('gx', 'gy'), may hold values from 0.3 to 1
- buoyancy: float32 [256, 256, 128], P('gx', 'gy'), may hold values from 0.5 to 1
- source_x: int32 [8], replicated, may hold values from 0 to 255
- source_y: int32 [8], replicated, may hold values from 0 to 255
- source_z: int32 [8], replicated, may hold values from 0 to 127
- source_wavelet: float32 [8], replicated, may hold values from -16 to 16
- receiver_x: int32 [256], replicated, may hold values from 0 to 255
- receiver_y: int32 [256], replicated, may hold values from 0 to 255
- receiver_residual: float32 [2, 256], replicated, may hold values from -16 to 16
- absorb_width: int32 [1], replicated, may hold values from 8 to 16
Outputs:
- grad_lambda: float32 [256, 256, 128], P('gx', 'gy')
- grad_mu: float32 [256, 256, 128], P('gx', 'gy')
- grad_density: float32 [256, 256, 128], P('gx', 'gy')
All inputs are finite; a program needn't handle non-finite values.
Results may differ from a plain program's by a relative error of at most 0.00002.
Values sent between devices are 32-bit elements; how exact they have to be, the bound alone decides.
A program may use at most 64 MiB of HBM per device.

v0:
```python
import jax
import jax.numpy as jnp
from jax import lax
from jax.sharding import PartitionSpec as P

REC_DEPTH = 6


COEFS = (1225.0 / 1024.0, -245.0 / 3072.0, 49.0 / 5120.0, -5.0 / 7168.0)
TIME_STEP = 0.2
DAMPING = 0.3


def with_halo(block, sides, width):
    for axis, dim in sides:
        count = lax.axis_size(axis)
        forward = [(i, i + 1) for i in range(count - 1)]
        backward = [(target, source) for source, target in forward]
        low = lax.ppermute(
            lax.slice_in_dim(block, block.shape[dim] - width, None, axis=dim), axis, forward
        )
        high = lax.ppermute(lax.slice_in_dim(block, 0, width, axis=dim), axis, backward)
        block = jnp.concatenate([low, block, high], axis=dim)
    return block


def window(padded, axis, offset, start, count):
    begin = list(start)
    begin[axis] = begin[axis] + offset
    return lax.slice(padded, begin, [b + c for b, c in zip(begin, count)])


def forward_diff(padded, axis, start, count):
    total = 0.0
    for order, coef in enumerate(COEFS, 1):
        total = total + coef * (
            window(padded, axis, order, start, count)
            - window(padded, axis, 1 - order, start, count)
        )
    return total


def backward_diff(padded, axis, start, count):
    total = 0.0
    for order, coef in enumerate(COEFS, 1):
        total = total + coef * (
            window(padded, axis, order - 1, start, count)
            - window(padded, axis, -order, start, count)
        )
    return total


def divergence(stress, start, count):
    sxx, syy, szz, sxy, sxz, syz = stress
    force_x = (
        forward_diff(sxx, 0, start, count)
        + backward_diff(sxy, 1, start, count)
        + backward_diff(sxz, 2, start, count)
    )
    force_y = (
        backward_diff(sxy, 0, start, count)
        + forward_diff(syy, 1, start, count)
        + backward_diff(syz, 2, start, count)
    )
    force_z = (
        backward_diff(sxz, 0, start, count)
        + backward_diff(syz, 1, start, count)
        + forward_diff(szz, 2, start, count)
    )
    return (force_x, force_y, force_z)


def strain(velocity, start, count):
    vel_x, vel_y, vel_z = velocity
    exx = backward_diff(vel_x, 0, start, count)
    eyy = backward_diff(vel_y, 1, start, count)
    ezz = backward_diff(vel_z, 2, start, count)
    exy = forward_diff(vel_x, 1, start, count) + forward_diff(vel_y, 0, start, count)
    exz = forward_diff(vel_x, 2, start, count) + forward_diff(vel_z, 0, start, count)
    eyz = forward_diff(vel_y, 2, start, count) + forward_diff(vel_z, 1, start, count)
    return (exx, eyy, ezz, exy, exz, eyz)


def update_stress(stress, rates, lame_lambda, lame_mu, damp):
    trace = rates[0] + rates[1] + rates[2]
    result = []
    for k in range(3):
        result.append(
            damp * (stress[k] + TIME_STEP * (lame_lambda * trace + 2.0 * lame_mu * rates[k]))
        )
    for k in range(3, 6):
        result.append(damp * (stress[k] + TIME_STEP * lame_mu * rates[k]))
    return result


def taper(dist, width):
    frac = jnp.maximum(width - dist.astype(jnp.float32), 0.0) / width
    return jnp.exp(-DAMPING * frac * frac)


def imaging(grads, rates, adjoint, vel_after, vel_before):
    exx, eyy, ezz, exy, exz, eyz = rates
    g_lambda = grads[0] + (exx + eyy + ezz) * (adjoint[3] + adjoint[4] + adjoint[5])
    g_mu = (
        grads[1]
        + 2.0 * (exx * adjoint[3] + eyy * adjoint[4] + ezz * adjoint[5])
        + exy * adjoint[6]
        + exz * adjoint[7]
        + eyz * adjoint[8]
    )
    g_rho = (
        grads[2]
        + (
            adjoint[0] * (vel_after[0] - vel_before[0])
            + adjoint[1] * (vel_after[1] - vel_before[1])
            + adjoint[2] * (vel_after[2] - vel_before[2])
        )
        / TIME_STEP
    )
    return (g_lambda, g_mu, g_rho)


def inject(field, local_x, local_y, local_z, amounts):
    cells_x, cells_y, depth = field.shape
    inside = (local_x >= 0) & (local_x < cells_x) & (local_y >= 0) & (local_y < cells_y)
    values = jnp.where(inside, amounts, 0.0)
    return field.at[
        jnp.clip(local_x, 0, cells_x - 1), jnp.clip(local_y, 0, cells_y - 1), local_z
    ].add(values)


def join_fields(pieces):
    return pieces[0]


def local(
    forward_state,
    adjoint_state,
    lame_lambda,
    lame_mu,
    buoyancy,
    source_x,
    source_y,
    source_z,
    source_wavelet,
    receiver_x,
    receiver_y,
    receiver_residual,
    absorb_width,
):
    cells_x, cells_y, depth = buoyancy.shape
    anchor_x = lax.axis_index("gx") * cells_x
    anchor_y = lax.axis_index("gy") * cells_y
    total_x = cells_x * lax.axis_size("gx")
    total_y = cells_y * lax.axis_size("gy")
    width = absorb_width[0].astype(jnp.float32)
    interior = (4, 4, 4)
    count = (cells_x, cells_y, depth)
    coord_x = anchor_x - 0 + jnp.arange(cells_x + 2 * 0, dtype=jnp.int32)
    coord_y = anchor_y - 0 + jnp.arange(cells_y + 2 * 0, dtype=jnp.int32)
    coord_z = jnp.arange(depth, dtype=jnp.int32)
    taper_x = taper(jnp.minimum(coord_x, total_x - 1 - coord_x), width)
    taper_y = taper(jnp.minimum(coord_y, total_y - 1 - coord_y), width)
    taper_z = taper(depth - 1 - coord_z, width)
    damp = taper_x[:, None, None] * taper_y[None, :, None] * taper_z[None, None, :]
    valid_x = ((coord_x >= 0) & (coord_x < total_x)).astype(jnp.float32)
    valid_y = ((coord_y >= 0) & (coord_y < total_y)).astype(jnp.float32)
    inside = valid_x[:, None, None] * valid_y[None, :, None] * jnp.ones((1, 1, depth), jnp.float32)
    damp_in = (damp, inside)[0]

    def advance(states):
        stacked = join_fields([state[3:] for state in states])
        stress_halo = with_halo(stacked, (("gx", 1), ("gy", 2)), 4)
        stress_pad = jnp.pad(stress_halo, ((0, 0), (0, 0), (0, 0), (4, 4)))
        member = 0
        force = divergence(tuple((stress_pad[k] for k in range(6))), interior, count)
        state = states[member]
        velocities = [
            jnp.stack([damp_in * (state[k] + TIME_STEP * buoyancy * force[k]) for k in range(3)])
        ]
        vel_halo = with_halo(join_fields(velocities), (("gx", 1), ("gy", 2)), 4)
        vel_pad = jnp.pad(vel_halo, ((0, 0), (0, 0), (0, 0), (4, 4)))
        member = 0
        rates = strain(tuple((vel_pad[3 * member + k] for k in range(3))), interior, count)
        results = [(rates, velocities[member])]
        return results

    depth_cells = jnp.full_like(receiver_x, REC_DEPTH)

    def finish_adjoint(state, rates, velocity, residual_row):
        stress = update_stress(
            [state[k] for k in range(3, 9)], rates, lame_lambda, lame_mu, damp_in
        )
        adj_vz = inject(
            velocity[2],
            receiver_x - anchor_x,
            receiver_y - anchor_y,
            depth_cells,
            TIME_STEP * residual_row,
        )
        return jnp.stack([velocity[0], velocity[1], adj_vz] + stress)

    rates_one, vel_one = advance([forward_state])[0]
    stress = update_stress(
        [forward_state[k] for k in range(3, 9)], rates_one, lame_lambda, lame_mu, damp_in
    )
    for k in range(3):
        stress[k] = inject(
            stress[k],
            source_x - anchor_x,
            source_y - anchor_y,
            source_z,
            TIME_STEP * source_wavelet,
        )
    state_one = jnp.concatenate([vel_one, jnp.stack(stress)])
    rates_two, vel_two = advance([state_one])[0]
    adj_rates, adj_vel = advance([adjoint_state])[0]
    adjoint_one = finish_adjoint(adjoint_state, adj_rates, adj_vel, receiver_residual[0])
    adj_rates, adj_vel = advance([adjoint_one])[0]
    adjoint_zero = finish_adjoint(adjoint_one, adj_rates, adj_vel, receiver_residual[1])
    zero = jnp.zeros((cells_x, cells_y, depth), jnp.float32)
    grads = (zero, zero, zero)
    grads = imaging(grads, rates_two, adjoint_one, vel_two, vel_one)
    grads = imaging(grads, rates_one, adjoint_zero, vel_one, forward_state[:3])
    return (grads[0], grads[1], grads[2])


def solution(mesh):
    return jax.shard_map(
        local,
        mesh=mesh,
        in_specs=(
            P(None, "gx", "gy", None),
            P(None, "gx", "gy", None),
            P("gx", "gy", None),
            P("gx", "gy", None),
            P("gx", "gy", None),
            P(),
            P(),
            P(),
            P(),
            P(),
            P(),
            P(),
            P(),
        ),
        out_specs=(P("gx", "gy", None), P("gx", "gy", None), P("gx", "gy", None)),
        check_vma=False,
    )
```

profile of v0, /device:TPU:270, one launch (start us, length us, event | category | flops | bytes accessed | tf_op | source)
XLA Modules:
  0.0 246.9 jit_solution(15585723764299827436)
XLA Ops:
  0.7 1.1 fusion.638
  1.8 1.9 collective-permute-start
  3.8 9.8 %collective-permute-start.1 = (f32[6,4,16,128]{3,2,1,0:T(8,128)S(1)}, f32[6,4,16,128]{3,2,1,0:T(8,128)S(1)}, u32[]{:S(2)}, u32[]{:S(2)}) collective-permute-start(f32[6,4,16,128]{3,2,1,0:T(8,128)S(1)} %get-tuple-element.91), channel_id=1, source_target_pairs={{16,0},{32,16},{48,32},{64,48},{80,64},{96,80},{112,96},{128,112},... | collective-permute-start | bytes 589832 | tf_op jit(solution)/shard_map/ppermute | solution.py:22
  13.6 1.7 fusion.639
  15.4 1.9 collective-permute-start.16
  17.3 9.7 %collective-permute-start.17 = (f32[6,4,16,128]{3,2,1,0:T(8,128)S(1)}, f32[6,4,16,128]{3,2,1,0:T(8,128)S(1)}, u32[]{:S(2)}, u32[]{:S(2)}) collective-permute-start(f32[6,4,16,128]{3,2,1,0:T(8,128)S(1)} %get-tuple-element.93), channel_id=1, source_target_pairs={{16,0},{32,16},{48,32},{64,48},{80,64},{96,80},{112,96},{128,112},... | collective-permute-start | bytes 589832 | tf_op jit(solution)/shard_map/ppermute | solution.py:22
  28.9 1.2 collective-permute-done.17
  30.2 8.0 %collective-permute-start.18 = (f32[6,16,4,128]{3,2,1,0:T(4,128)S(1)}, f32[6,16,4,128]{3,2,1,0:T(4,128)S(1)}, u32[]{:S(2)}, u32[]{:S(2)}) collective-permute-start(f32[6,16,4,128]{3,2,1,0:T(4,128)S(1)} %get-tuple-element.86), channel_id=1, source_target_pairs={{0,1},{1,2},{2,3},{3,4},{4,5},{5,6},{6,7},{7,8},{8,9},{9,10},{10,1... | collective-permute-start | bytes 589832 | tf_op jit(solution)/shard_map/ppermute | solution.py:19
  38.2 1.9 collective-permute-start.19
  40.3 6.0 %collective-permute-start.2 = (f32[6,16,4,128]{3,2,1,0:T(4,128)S(1)}, f32[6,16,4,128]{3,2,1,0:T(4,128)S(1)}, u32[]{:S(2)}, u32[]{:S(2)}) collective-permute-start(f32[6,16,4,128]{3,2,1,0:T(4,128)S(1)} %get-tuple-element.84), channel_id=1, source_target_pairs={{0,1},{1,2},{2,3},{3,4},{4,5},{5,6},{6,7},{7,8},{8,9},{9,10},{10,1... | collective-permute-start | bytes 589832 | tf_op jit(solution)/shard_map/ppermute | solution.py:19
  46.3 1.9 collective-permute-start.3
  51.7 1.9 collective-permute-start.20
  53.7 9.7 %collective-permute-start.21 = (f32[3,4,16,128]{3,2,1,0:T(8,128)S(1)}, f32[3,4,16,128]{3,2,1,0:T(8,128)S(1)}, u32[]{:S(2)}, u32[]{:S(2)}) collective-permute-start(f32[3,4,16,128]{3,2,1,0:T(8,128)S(1)} %get-tuple-element.113), channel_id=1, source_target_pairs={{16,0},{32,16},{48,32},{64,48},{80,64},{96,80},{112,96},{128,112},... | collective-permute-start | bytes 294920 | tf_op jit(solution)/shard_map/ppermute | solution.py:22
  66.2 1.9 collective-permute-start.4
  68.2 9.7 %collective-permute-start.5 = (f32[3,4,16,128]{3,2,1,0:T(8,128)S(1)}, f32[3,4,16,128]{3,2,1,0:T(8,128)S(1)}, u32[]{:S(2)}, u32[]{:S(2)}) collective-permute-start(f32[3,4,16,128]{3,2,1,0:T(8,128)S(1)} %get-tuple-element.111), channel_id=1, source_target_pairs={{16,0},{32,16},{48,32},{64,48},{80,64},{96,80},{112,96},{128,112},... | collective-permute-start | bytes 294920 | tf_op jit(solution)/shard_map/ppermute | solution.py:22
  77.9 6.0 %collective-permute-start.22 = (f32[3,16,4,128]{3,2,1,0:T(4,128)S(1)}, f32[3,16,4,128]{3,2,1,0:T(4,128)S(1)}, u32[]{:S(2)}, u32[]{:S(2)}) collective-permute-start(f32[3,16,4,128]{3,2,1,0:T(4,128)S(1)} %get-tuple-element.104), channel_id=1, source_target_pairs={{0,1},{1,2},{2,3},{3,4},{4,5},{5,6},{6,7},{7,8},{8,9},{9,10},{10,1... | collective-permute-start | bytes 294920 | tf_op jit(solution)/shard_map/ppermute | solution.py:19
  83.9 1.9 collective-permute-start.23
  85.9 6.0 %collective-permute-start.6 = (f32[3,16,4,128]{3,2,1,0:T(4,128)S(1)}, f32[3,16,4,128]{3,2,1,0:T(4,128)S(1)}, u32[]{:S(2)}, u32[]{:S(2)}) collective-permute-start(f32[3,16,4,128]{3,2,1,0:T(4,128)S(1)} %get-tuple-element.102), channel_id=1, source_target_pairs={{0,1},{1,2},{2,3},{3,4},{4,5},{5,6},{6,7},{7,8},{8,9},{9,10},{10,1... | collective-permute-start | bytes 294920 | tf_op jit(solution)/shard_map/ppermute | solution.py:19
  92.0 1.9 collective-permute-start.7
  95.4 1.1 bitcast_dynamic-update-slice_fusion.5
  101.6 1.9 collective-permute-start.24
  103.6 9.8 %collective-permute-start.25 = (f32[6,4,16,128]{3,2,1,0:T(8,128)}, f32[6,4,16,128]{3,2,1,0:T(8,128)}, u32[]{:S(2)}, u32[]{:S(2)}) collective-permute-start(f32[6,4,16,128]{3,2,1,0:T(8,128)} %get-tuple-element.101), channel_id=1, source_target_pairs={{16,0},{32,16},{48,32},{64,48},{80,64},{96,80},{112,96},{128,112},... | collective-permute-start | bytes 589832 | tf_op jit(solution)/shard_map/ppermute | solution.py:22
  114.1 1.1 multiply_multiply_fusion.24
  121.8 1.9 collective-permute-start.8
  123.7 9.7 %collective-permute-start.9 = (f32[6,4,16,128]{3,2,1,0:T(8,128)S(1)}, f32[6,4,16,128]{3,2,1,0:T(8,128)S(1)}, u32[]{:S(2)}, u32[]{:S(2)}) collective-permute-start(f32[6,4,16,128]{3,2,1,0:T(8,128)S(1)} %get-tuple-element.99), channel_id=1, source_target_pairs={{16,0},{32,16},{48,32},{64,48},{80,64},{96,80},{112,96},{128,112},... | collective-permute-start | bytes 589832 | tf_op jit(solution)/shard_map/ppermute | solution.py:22
  133.4 1.1 pad_maximum_fusion.2
  134.5 6.0 %collective-permute-start.26 = (f32[6,16,4,128]{3,2,1,0:T(4,128)S(1)}, f32[6,16,4,128]{3,2,1,0:T(4,128)S(1)}, u32[]{:S(2)}, u32[]{:S(2)}) collective-permute-start(f32[6,16,4,128]{3,2,1,0:T(4,128)S(1)} %get-tuple-element.82), channel_id=1, source_target_pairs={{0,1},{1,2},{2,3},{3,4},{4,5},{5,6},{6,7},{7,8},{8,9},{9,10},{10,1... | collective-permute-start | bytes 589832 | tf_op jit(solution)/shard_map/ppermute | solution.py:19
  140.6 1.9 collective-permute-start.27
  142.5 15.4 %scatter_fusion.3 = f32[8,16,128]{2,1,0:T(8,128)S(1)} fusion(f32[8,16,128]{2,1,0:T(8,128)S(1)} %multiply_multiply_fusion.15, s32[256]{0:T(256)S(1)} %bitcast.221, f32[256]{0:T(256)S(1)} %broadcast_select_fusion.1), kind=kCustom, calls=%fused_computation.3 | custom fusion | flops 256 | bytes 6144 | tf_op jit(solution)/shard_map/scatter-add | solution.py:129
  158.0 6.0 %collective-permute-start.10 = (f32[6,16,4,128]{3,2,1,0:T(4,128)S(1)}, f32[6,16,4,128]{3,2,1,0:T(4,128)S(1)}, u32[]{:S(2)}, u32[]{:S(2)}) collective-permute-start(f32[6,16,4,128]{3,2,1,0:T(4,128)S(1)} %get-tuple-element.80), channel_id=1, source_target_pairs={{0,1},{1,2},{2,3},{3,4},{4,5},{5,6},{6,7},{7,8},{8,9},{9,10},{10,1... | collective-permute-start | bytes 589832 | tf_op jit(solution)/shard_map/ppermute | solution.py:19
  164.1 1.9 collective-permute-start.11
  166.0 2.1 select_maximum_fusion
  168.1 1.2 slice_bitcast_fusion.5
  169.8 3.9 %collective-permute-done.11 = f32[6,16,4,128]{3,2,1,0:T(4,128)S(1)} collective-permute-done((f32[6,16,4,128]{3,2,1,0:T(4,128)S(1)}, f32[6,16,4,128]{3,2,1,0:T(4,128)S(1)}, u32[]{:S(2)}, u32[]{:S(2)}) %collective-permute-start.11) | collective-permute-done | bytes 196640 | tf_op jit(solution)/shard_map/ppermute | solution.py:22
  174.8 1.1 slice_bitcast_fusion.21
  176.0 15.4 %scatter_fusion.4 = f32[8,16,128]{2,1,0:T(8,128)S(1)} fusion(f32[8,16,128]{2,1,0:T(8,128)S(1)} %copy.30, s32[256]{0:T(256)S(1)} %bitcast.222, f32[256]{0:T(256)S(1)} %get-tuple-element.9), kind=kCustom, calls=%fused_computation.4 | custom fusion | flops 256 | bytes 6144 | tf_op jit(solution)/shard_map/scatter-add | solution.py:129
  191.4 6.5 %fusion.600 = (f32[8,16,128]{2,1,0:T(8,128)}, f32[8,16,128]{2,1,0:T(8,128)S(1)}, f32[8,16,128]{2,1,0:T(8,128)S(1)}, f32[8,16,128]{2,1,0:T(8,128)S(1)}, f32[8,16,128]{2,1,0:T(8,128)S(1)}, /*index=5*/f32[8,16,128]{2,1,0:T(8,128)S(1)}) fusion(f32[8,16,128]{2,1,0:T(8,128)S(1)} %scatter_fusion.4, f32[8,16,128]{2,1,0:T(8,128)S(1)} %multiply_multiply_fusion.27, ...), kind=kLoop, calls=%fused_computation.1057 | loop fusion | flops 3440640 | bytes 8717312 | tf_op jit(solution)/shard_map/add | solution.py:112
  197.9 1.9 collective-permute-start.28
  199.9 9.7 %collective-permute-start.29 = (f32[3,4,16,128]{3,2,1,0:T(8,128)S(1)}, f32[3,4,16,128]{3,2,1,0:T(8,128)S(1)}, u32[]{:S(2)}, u32[]{:S(2)}) collective-permute-start(f32[3,4,16,128]{3,2,1,0:T(8,128)S(1)} %get-tuple-element.109), channel_id=1, source_target_pairs={{16,0},{32,16},{48,32},{64,48},{80,64},{96,80},{112,96},{128,112},... | collective-permute-start | bytes 294920 | tf_op jit(solution)/shard_map/ppermute | solution.py:22
  209.6 1.9 collective-permute-start.12
  211.5 9.7 %collective-permute-start.13 = (f32[3,4,16,128]{3,2,1,0:T(8,128)S(1)}, f32[3,4,16,128]{3,2,1,0:T(8,128)S(1)}, u32[]{:S(2)}, u32[]{:S(2)}) collective-permute-start(f32[3,4,16,128]{3,2,1,0:T(8,128)S(1)} %get-tuple-element.107), channel_id=1, source_target_pairs={{16,0},{32,16},{48,32},{64,48},{80,64},{96,80},{112,96},{128,112},... | collective-permute-start | bytes 294920 | tf_op jit(solution)/shard_map/ppermute | solution.py:22
  221.2 2.7 %collective-permute-start.30 = (f32[3,16,4,128]{3,2,1,0:T(4,128)S(1)}, f32[3,16,4,128]{3,2,1,0:T(4,128)S(1)}, u32[]{:S(2)}, u32[]{:S(2)}) collective-permute-start(f32[3,16,4,128]{3,2,1,0:T(4,128)S(1)} %get-tuple-element.96), channel_id=1, source_target_pairs={{0,1},{1,2},{2,3},{3,4},{4,5},{5,6},{6,7},{7,8},{8,9},{9,10},{10,1... | collective-permute-start | bytes 294920 | tf_op jit(solution)/shard_map/ppermute | solution.py:19
  224.0 3.1 %collective-permute-start.31 = (f32[3,16,4,128]{3,2,1,0:T(4,128)S(1)}, f32[3,16,4,128]{3,2,1,0:T(4,128)S(1)}, u32[]{:S(2)}, u32[]{:S(2)}) collective-permute-start(f32[3,16,4,128]{3,2,1,0:T(4,128)S(1)} %get-tuple-element.97), channel_id=1, source_target_pairs={{1,0},{2,1},{3,2},{4,3},{5,4},{6,5},{7,6},{8,7},{9,8},{10,9},{11,1... | collective-permute-start | bytes 294920 | tf_op jit(solution)/shard_map/ppermute | solution.py:22
  227.2 4.8 %collective-permute-start.14 = (f32[3,16,4,128]{3,2,1,0:T(4,128)S(1)}, f32[3,16,4,128]{3,2,1,0:T(4,128)S(1)}, u32[]{:S(2)}, u32[]{:S(2)}) collective-permute-start(f32[3,16,4,128]{3,2,1,0:T(4,128)S(1)} %get-tuple-element.94), channel_id=1, source_target_pairs={{0,1},{1,2},{2,3},{3,4},{4,5},{5,6},{6,7},{7,8},{8,9},{9,10},{10,1... | collective-permute-start | bytes 294920 | tf_op jit(solution)/shard_map/ppermute | solution.py:19
  232.0 2.1 collective-permute-start.15
  234.8 5.8 %collective-permute-done.15 = f32[3,16,4,128]{3,2,1,0:T(4,128)S(1)} collective-permute-done((f32[3,16,4,128]{3,2,1,0:T(4,128)S(1)}, f32[3,16,4,128]{3,2,1,0:T(4,128)S(1)}, u32[]{:S(2)}, u32[]{:S(2)}) %collective-permute-start.15) | collective-permute-done | bytes 98336 | tf_op jit(solution)/shard_map/ppermute | solution.py:22
  242.4 2.9 %fusion.11 = (f32[8,16,128]{2,1,0:T(8,128)}, f32[8,16,128]{2,1,0:T(8,128)S(1)}, f32[8,16,128]{2,1,0:T(8,128)S(1)}, f32[8,16,128]{2,1,0:T(8,128)S(1)}, f32[8,16,1...) fusion(f32[8,16,128]{2,1,0:T(8,128)S(1)} %copy-done.19, f32[8,16,128]{2,1,0:T(8,128)S(1)} %copy-done.20, ...), kind=kLoop, calls=%fused_computation.162 | loop fusion | flops 4243456 | bytes 10028032 | tf_op jit(solution)/shard_map/add | solution.py:105
  245.3 1.6 multiply_add_fusion
  (154 shorter events, 25.7 us)
Async XLA Ops:
  0.6 26.3 %copy-start.1 = (f32[9,8,16,128]{3,2,1,0:T(8,128)S(1)}, f32[9,8,16,128]{3,2,1,0:T(8,128)}, u32[]{:S(2)}) copy-start(f32[9,8,16,128]{3,2,1,0:T(8,128)} %param.13) | copy-start | bytes 1769476
  0.6 26.4 %copy-start.3 = (f32[9,8,16,128]{3,2,1,0:T(8,128)S(1)}, f32[9,8,16,128]{3,2,1,0:T(8,128)}, u32[]{:S(2)}) copy-start(f32[9,8,16,128]{3,2,1,0:T(8,128)} %param.14) | copy-start | bytes 1769476
  1.8 38.4 %collective-permute-start = (f32[6,4,16,128]{3,2,1,0:T(8,128)S(1)}, f32[6,4,16,128]{3,2,1,0:T(8,128)S(1)}, u32[]{:S(2)}, u32[]{:S(2)}) collective-permute-start(f32[6,4,16,128]{3,2,1,0:T(8,128)S(1)} %get-tuple-element.90), channel_id=1, source_target_pairs={{0,16},{16,32},{32,48},{48,64},{64,80},{80,96},{96,112},{112,128},... | collective-permute-start | bytes 589832 | tf_op jit(solution)/shard_map/ppermute | solution.py:19
  3.7 24.0 %copy-start.23 = (s32[256]{0:T(256)S(1)}, s32[256]{0:T(256)}, u32[]{:S(2)}) copy-start(s32[256]{0:T(256)} %param.22) | copy-start | bytes 3076
  3.7 24.0 %copy-start.22 = (s32[256]{0:T(256)S(1)}, s32[256]{0:T(256)}, u32[]{:S(2)}) copy-start(s32[256]{0:T(256)} %param.23) | copy-start | bytes 3076
  3.8 24.0 %copy-start.24 = (f32[2,256]{1,0:T(2,128)S(1)}, f32[2,256]{1,0:T(2,128)}, u32[]{:S(2)}) copy-start(f32[2,256]{1,0:T(2,128)} %param.24) | copy-start | bytes 6148
  3.8 24.1 %copy-start.25 = (s32[8]{0:T(128)S(1)}, s32[8]{0:T(128)}, u32[]{:S(2)}) copy-start(s32[8]{0:T(128)} %param.19) | copy-start | bytes 100
  3.8 24.1 %copy-start.26 = (s32[8]{0:T(128)S(1)}, s32[8]{0:T(128)}, u32[]{:S(2)}) copy-start(s32[8]{0:T(128)} %param.18) | copy-start | bytes 100
  3.8 24.1 %copy-start.27 = (s32[8]{0:T(128)S(1)}, s32[8]{0:T(128)}, u32[]{:S(2)}) copy-start(s32[8]{0:T(128)} %param.20) | copy-start | bytes 100
  3.8 24.1 %copy-start.28 = (f32[8]{0:T(128)S(1)}, f32[8]{0:T(128)}, u32[]{:S(2)}) copy-start(f32[8]{0:T(128)} %param.21) | copy-start | bytes 100
  3.8 36.4 %collective-permute-start.1 = (f32[6,4,16,128]{3,2,1,0:T(8,128)S(1)}, f32[6,4,16,128]{3,2,1,0:T(8,128)S(1)}, u32[]{:S(2)}, u32[]{:S(2)}) collective-permute-start(f32[6,4,16,128]{3,2,1,0:T(8,128)S(1)} %get-tuple-element.91), channel_id=1, source_target_pairs={{16,0},{32,16},{48,32},{64,48},{80,64},{96,80},{112,96},{128,112},... | collective-permute-start | bytes 589832 | tf_op jit(solution)/shard_map/ppermute | solution.py:22
  15.4 13.5 %collective-permute-start.16 = (f32[6,4,16,128]{3,2,1,0:T(8,128)}, f32[6,4,16,128]{3,2,1,0:T(8,128)S(1)}, u32[]{:S(2)}, u32[]{:S(2)}) collective-permute-start(f32[6,4,16,128]{3,2,1,0:T(8,128)} %get-tuple-element.92), channel_id=1, source_target_pairs={{0,16},{16,32},{32,48},{48,64},{64,80},{80,96},{96,112},{112,128},... | collective-permute-start | bytes 589832 | tf_op jit(solution)/shard_map/ppermute | solution.py:19
  17.3 12.8 %collective-permute-start.17 = (f32[6,4,16,128]{3,2,1,0:T(8,128)S(1)}, f32[6,4,16,128]{3,2,1,0:T(8,128)S(1)}, u32[]{:S(2)}, u32[]{:S(2)}) collective-permute-start(f32[6,4,16,128]{3,2,1,0:T(8,128)S(1)} %get-tuple-element.93), channel_id=1, source_target_pairs={{16,0},{32,16},{48,32},{64,48},{80,64},{96,80},{112,96},{128,112},... | collective-permute-start | bytes 589832 | tf_op jit(solution)/shard_map/ppermute | solution.py:22
  30.2 18.1 %collective-permute-start.18 = (f32[6,16,4,128]{3,2,1,0:T(4,128)S(1)}, f32[6,16,4,128]{3,2,1,0:T(4,128)S(1)}, u32[]{:S(2)}, u32[]{:S(2)}) collective-permute-start(f32[6,16,4,128]{3,2,1,0:T(4,128)S(1)} %get-tuple-element.86), channel_id=1, source_target_pairs={{0,1},{1,2},{2,3},{3,4},{4,5},{5,6},{6,7},{7,8},{8,9},{9,10},{10,1... | collective-permute-start | bytes 589832 | tf_op jit(solution)/shard_map/ppermute | solution.py:19
  38.2 10.0 %collective-permute-start.19 = (f32[6,16,4,128]{3,2,1,0:T(4,128)S(1)}, f32[6,16,4,128]{3,2,1,0:T(4,128)S(1)}, u32[]{:S(2)}, u32[]{:S(2)}) collective-permute-start(f32[6,16,4,128]{3,2,1,0:T(4,128)S(1)} %get-tuple-element.87), channel_id=1, source_target_pairs={{1,0},{2,1},{3,2},{4,3},{5,4},{6,5},{7,6},{8,7},{9,8},{10,9},{11,1... | collective-permute-start | bytes 589832 | tf_op jit(solution)/shard_map/ppermute | solution.py:22
  40.3 23.1 %collective-permute-start.2 = (f32[6,16,4,128]{3,2,1,0:T(4,128)S(1)}, f32[6,16,4,128]{3,2,1,0:T(4,128)S(1)}, u32[]{:S(2)}, u32[]{:S(2)}) collective-permute-start(f32[6,16,4,128]{3,2,1,0:T(4,128)S(1)} %get-tuple-element.84), channel_id=1, source_target_pairs={{0,1},{1,2},{2,3},{3,4},{4,5},{5,6},{6,7},{7,8},{8,9},{9,10},{10,1... | collective-permute-start | bytes 589832 | tf_op jit(solution)/shard_map/ppermute | solution.py:19
  46.3 17.0 %collective-permute-start.3 = (f32[6,16,4,128]{3,2,1,0:T(4,128)S(1)}, f32[6,16,4,128]{3,2,1,0:T(4,128)S(1)}, u32[]{:S(2)}, u32[]{:S(2)}) collective-permute-start(f32[6,16,4,128]{3,2,1,0:T(4,128)S(1)} %get-tuple-element.85), channel_id=1, source_target_pairs={{1,0},{2,1},{3,2},{4,3},{5,4},{6,5},{7,6},{8,7},{9,8},{10,9},{11,1... | collective-permute-start | bytes 589832 | tf_op jit(solution)/shard_map/ppermute | solution.py:22
  51.7 26.1 %collective-permute-start.20 = (f32[3,4,16,128]{3,2,1,0:T(8,128)S(1)}, f32[3,4,16,128]{3,2,1,0:T(8,128)S(1)}, u32[]{:S(2)}, u32[]{:S(2)}) collective-permute-start(f32[3,4,16,128]{3,2,1,0:T(8,128)S(1)} %get-tuple-element.112), channel_id=1, source_target_pairs={{0,16},{16,32},{32,48},{48,64},{64,80},{80,96},{96,112},{112,128},... | collective-permute-start | bytes 294920 | tf_op jit(solution)/shard_map/ppermute | solution.py:19
  53.7 24.2 %collective-permute-start.21 = (f32[3,4,16,128]{3,2,1,0:T(8,128)S(1)}, f32[3,4,16,128]{3,2,1,0:T(8,128)S(1)}, u32[]{:S(2)}, u32[]{:S(2)}) collective-permute-start(f32[3,4,16,128]{3,2,1,0:T(8,128)S(1)} %get-tuple-element.113), channel_id=1, source_target_pairs={{16,0},{32,16},{48,32},{64,48},{80,64},{96,80},{112,96},{128,112},... | collective-permute-start | bytes 294920 | tf_op jit(solution)/shard_map/ppermute | solution.py:22
  66.2 19.6 %collective-permute-start.4 = (f32[3,4,16,128]{3,2,1,0:T(8,128)S(1)}, f32[3,4,16,128]{3,2,1,0:T(8,128)S(1)}, u32[]{:S(2)}, u32[]{:S(2)}) collective-permute-start(f32[3,4,16,128]{3,2,1,0:T(8,128)S(1)} %get-tuple-element.110), channel_id=1, source_target_pairs={{0,16},{16,32},{32,48},{48,64},{64,80},{80,96},{96,112},{112,128},... | collective-permute-start | bytes 294920 | tf_op jit(solution)/shard_map/ppermute | solution.py:19
  68.2 17.7 %collective-permute-start.5 = (f32[3,4,16,128]{3,2,1,0:T(8,128)S(1)}, f32[3,4,16,128]{3,2,1,0:T(8,128)S(1)}, u32[]{:S(2)}, u32[]{:S(2)}) collective-permute-start(f32[3,4,16,128]{3,2,1,0:T(8,128)S(1)} %get-tuple-element.111), channel_id=1, source_target_pairs={{16,0},{32,16},{48,32},{64,48},{80,64},{96,80},{112,96},{128,112},... | collective-permute-start | bytes 294920 | tf_op jit(solution)/shard_map/ppermute | solution.py:22
  77.9 16.0 %collective-permute-start.22 = (f32[3,16,4,128]{3,2,1,0:T(4,128)S(1)}, f32[3,16,4,128]{3,2,1,0:T(4,128)S(1)}, u32[]{:S(2)}, u32[]{:S(2)}) collective-permute-start(f32[3,16,4,128]{3,2,1,0:T(4,128)S(1)} %get-tuple-element.104), channel_id=1, source_target_pairs={{0,1},{1,2},{2,3},{3,4},{4,5},{5,6},{6,7},{7,8},{8,9},{9,10},{10,1... | collective-permute-start | bytes 294920 | tf_op jit(solution)/shard_map/ppermute | solution.py:19
  83.9 10.0 %collective-permute-start.23 = (f32[3,16,4,128]{3,2,1,0:T(4,128)S(1)}, f32[3,16,4,128]{3,2,1,0:T(4,128)S(1)}, u32[]{:S(2)}, u32[]{:S(2)}) collective-permute-start(f32[3,16,4,128]{3,2,1,0:T(4,128)S(1)} %get-tuple-element.105), channel_id=1, source_target_pairs={{1,0},{2,1},{3,2},{4,3},{5,4},{6,5},{7,6},{8,7},{9,8},{10,9},{11,1... | collective-permute-start | bytes 294920 | tf_op jit(solution)/shard_map/ppermute | solution.py:22
  85.9 27.5 %collective-permute-start.6 = (f32[3,16,4,128]{3,2,1,0:T(4,128)S(1)}, f32[3,16,4,128]{3,2,1,0:T(4,128)S(1)}, u32[]{:S(2)}, u32[]{:S(2)}) collective-permute-start(f32[3,16,4,128]{3,2,1,0:T(4,128)S(1)} %get-tuple-element.102), channel_id=1, source_target_pairs={{0,1},{1,2},{2,3},{3,4},{4,5},{5,6},{6,7},{7,8},{8,9},{9,10},{10,1... | collective-permute-start | bytes 294920 | tf_op jit(solution)/shard_map/ppermute | solution.py:19
  92.0 21.5 %collective-permute-start.7 = (f32[3,16,4,128]{3,2,1,0:T(4,128)S(1)}, f32[3,16,4,128]{3,2,1,0:T(4,128)S(1)}, u32[]{:S(2)}, u32[]{:S(2)}) collective-permute-start(f32[3,16,4,128]{3,2,1,0:T(4,128)S(1)} %get-tuple-element.103), channel_id=1, source_target_pairs={{1,0},{2,1},{3,2},{4,3},{5,4},{6,5},{7,6},{8,7},{9,8},{10,9},{11,1... | collective-permute-start | bytes 294920 | tf_op jit(solution)/shard_map/ppermute | solution.py:22
  101.6 31.7 %collective-permute-start.24 = (f32[6,4,16,128]{3,2,1,0:T(8,128)}, f32[6,4,16,128]{3,2,1,0:T(8,128)}, u32[]{:S(2)}, u32[]{:S(2)}) collective-permute-start(f32[6,4,16,128]{3,2,1,0:T(8,128)} %get-tuple-element.100), channel_id=1, source_target_pairs={{0,16},{16,32},{32,48},{48,64},{64,80},{80,96},{96,112},{112,128},... | collective-permute-start | bytes 589832 | tf_op jit(solution)/shard_map/ppermute | solution.py:19
  103.6 29.8 %collective-permute-start.25 = (f32[6,4,16,128]{3,2,1,0:T(8,128)}, f32[6,4,16,128]{3,2,1,0:T(8,128)}, u32[]{:S(2)}, u32[]{:S(2)}) collective-permute-start(f32[6,4,16,128]{3,2,1,0:T(8,128)} %get-tuple-element.101), channel_id=1, source_target_pairs={{16,0},{32,16},{48,32},{64,48},{80,64},{96,80},{112,96},{128,112},... | collective-permute-start | bytes 589832 | tf_op jit(solution)/shard_map/ppermute | solution.py:22
  115.2 1.9 copy-start.8
  115.2 2.0 copy-start.10
  121.8 36.1 %collective-permute-start.8 = (f32[6,4,16,128]{3,2,1,0:T(8,128)}, f32[6,4,16,128]{3,2,1,0:T(8,128)S(1)}, u32[]{:S(2)}, u32[]{:S(2)}) collective-permute-start(f32[6,4,16,128]{3,2,1,0:T(8,128)} %get-tuple-element.98), channel_id=1, source_target_pairs={{0,16},{16,32},{32,48},{48,64},{64,80},{80,96},{96,112},{112,128},... | collective-permute-start | bytes 589832 | tf_op jit(solution)/shard_map/ppermute | solution.py:19
  123.7 34.2 %collective-permute-start.9 = (f32[6,4,16,128]{3,2,1,0:T(8,128)S(1)}, f32[6,4,16,128]{3,2,1,0:T(8,128)S(1)}, u32[]{:S(2)}, u32[]{:S(2)}) collective-permute-start(f32[6,4,16,128]{3,2,1,0:T(8,128)S(1)} %get-tuple-element.99), channel_id=1, source_target_pairs={{16,0},{32,16},{48,32},{64,48},{80,64},{96,80},{112,96},{128,112},... | collective-permute-start | bytes 589832 | tf_op jit(solution)/shard_map/ppermute | solution.py:22
  134.5 31.5 %collective-permute-start.26 = (f32[6,16,4,128]{3,2,1,0:T(4,128)S(1)}, f32[6,16,4,128]{3,2,1,0:T(4,128)S(1)}, u32[]{:S(2)}, u32[]{:S(2)}) collective-permute-start(f32[6,16,4,128]{3,2,1,0:T(4,128)S(1)} %get-tuple-element.82), channel_id=1, source_target_pairs={{0,1},{1,2},{2,3},{3,4},{4,5},{5,6},{6,7},{7,8},{8,9},{9,10},{10,1... | collective-permute-start | bytes 589832 | tf_op jit(solution)/shard_map/ppermute | solution.py:19
  140.6 25.4 %collective-permute-start.27 = (f32[6,16,4,128]{3,2,1,0:T(4,128)S(1)}, f32[6,16,4,128]{3,2,1,0:T(4,128)S(1)}, u32[]{:S(2)}, u32[]{:S(2)}) collective-permute-start(f32[6,16,4,128]{3,2,1,0:T(4,128)S(1)} %get-tuple-element.83), channel_id=1, source_target_pairs={{1,0},{2,1},{3,2},{4,3},{5,4},{6,5},{7,6},{8,7},{9,8},{10,9},{11,1... | collective-permute-start | bytes 589832 | tf_op jit(solution)/shard_map/ppermute | solution.py:22
  158.0 11.8 %collective-permute-start.10 = (f32[6,16,4,128]{3,2,1,0:T(4,128)S(1)}, f32[6,16,4,128]{3,2,1,0:T(4,128)S(1)}, u32[]{:S(2)}, u32[]{:S(2)}) collective-permute-start(f32[6,16,4,128]{3,2,1,0:T(4,128)S(1)} %get-tuple-element.80), channel_id=1, source_target_pairs={{0,1},{1,2},{2,3},{3,4},{4,5},{5,6},{6,7},{7,8},{8,9},{9,10},{10,1... | collective-permute-start | bytes 589832 | tf_op jit(solution)/shard_map/ppermute | solution.py:19
  164.1 9.7 %collective-permute-start.11 = (f32[6,16,4,128]{3,2,1,0:T(4,128)S(1)}, f32[6,16,4,128]{3,2,1,0:T(4,128)S(1)}, u32[]{:S(2)}, u32[]{:S(2)}) collective-permute-start(f32[6,16,4,128]{3,2,1,0:T(4,128)S(1)} %get-tuple-element.81), channel_id=1, source_target_pairs={{1,0},{2,1},{3,2},{4,3},{5,4},{6,5},{7,6},{8,7},{9,8},{10,9},{11,1... | collective-permute-start | bytes 589832 | tf_op jit(solution)/shard_map/ppermute | solution.py:22
  169.8 3.9 %copy-start.4 = (f32[8,16,128]{2,1,0:T(8,128)}, f32[8,16,128]{2,1,0:T(8,128)S(1)}, u32[]{:S(2)}) copy-start(f32[8,16,128]{2,1,0:T(8,128)S(1)} %multiply_multiply_fusion.6) | copy-start | bytes 196612
  191.4 6.5 %copy-start.5 = (f32[8,16,128]{2,1,0:T(8,128)S(1)}, f32[8,16,128]{2,1,0:T(8,128)}, u32[]{:S(2)}) copy-start(f32[8,16,128]{2,1,0:T(8,128)} %copy-done.4) | copy-start | bytes 196612
  197.9 23.2 %collective-permute-start.28 = (f32[3,4,16,128]{3,2,1,0:T(8,128)S(1)}, f32[3,4,16,128]{3,2,1,0:T(8,128)S(1)}, u32[]{:S(2)}, u32[]{:S(2)}) collective-permute-start(f32[3,4,16,128]{3,2,1,0:T(8,128)S(1)} %get-tuple-element.108), channel_id=1, source_target_pairs={{0,16},{16,32},{32,48},{48,64},{64,80},{80,96},{96,112},{112,128},... | collective-permute-start | bytes 294920 | tf_op jit(solution)/shard_map/ppermute | solution.py:19
  199.9 21.3 %collective-permute-start.29 = (f32[3,4,16,128]{3,2,1,0:T(8,128)S(1)}, f32[3,4,16,128]{3,2,1,0:T(8,128)S(1)}, u32[]{:S(2)}, u32[]{:S(2)}) collective-permute-start(f32[3,4,16,128]{3,2,1,0:T(8,128)S(1)} %get-tuple-element.109), channel_id=1, source_target_pairs={{16,0},{32,16},{48,32},{64,48},{80,64},{96,80},{112,96},{128,112},... | collective-permute-start | bytes 294920 | tf_op jit(solution)/shard_map/ppermute | solution.py:22
  209.6 17.5 %collective-permute-start.12 = (f32[3,4,16,128]{3,2,1,0:T(8,128)S(1)}, f32[3,4,16,128]{3,2,1,0:T(8,128)S(1)}, u32[]{:S(2)}, u32[]{:S(2)}) collective-permute-start(f32[3,4,16,128]{3,2,1,0:T(8,128)S(1)} %get-tuple-element.106), channel_id=1, source_target_pairs={{0,16},{16,32},{32,48},{48,64},{64,80},{80,96},{96,112},{112,128},... | collective-permute-start | bytes 294920 | tf_op jit(solution)/shard_map/ppermute | solution.py:19
  211.5 15.6 %collective-permute-start.13 = (f32[3,4,16,128]{3,2,1,0:T(8,128)S(1)}, f32[3,4,16,128]{3,2,1,0:T(8,128)S(1)}, u32[]{:S(2)}, u32[]{:S(2)}) collective-permute-start(f32[3,4,16,128]{3,2,1,0:T(8,128)S(1)} %get-tuple-element.107), channel_id=1, source_target_pairs={{16,0},{32,16},{48,32},{64,48},{80,64},{96,80},{112,96},{128,112},... | collective-permute-start | bytes 294920 | tf_op jit(solution)/shard_map/ppermute | solution.py:22
  221.2 12.9 %collective-permute-start.30 = (f32[3,16,4,128]{3,2,1,0:T(4,128)S(1)}, f32[3,16,4,128]{3,2,1,0:T(4,128)S(1)}, u32[]{:S(2)}, u32[]{:S(2)}) collective-permute-start(f32[3,16,4,128]{3,2,1,0:T(4,128)S(1)} %get-tuple-element.96), channel_id=1, source_target_pairs={{0,1},{1,2},{2,3},{3,4},{4,5},{5,6},{6,7},{7,8},{8,9},{9,10},{10,1... | collective-permute-start | bytes 294920 | tf_op jit(solution)/shard_map/ppermute | solution.py:19
  224.0 10.2 %collective-permute-start.31 = (f32[3,16,4,128]{3,2,1,0:T(4,128)S(1)}, f32[3,16,4,128]{3,2,1,0:T(4,128)S(1)}, u32[]{:S(2)}, u32[]{:S(2)}) collective-permute-start(f32[3,16,4,128]{3,2,1,0:T(4,128)S(1)} %get-tuple-element.97), channel_id=1, source_target_pairs={{1,0},{2,1},{3,2},{4,3},{5,4},{6,5},{7,6},{8,7},{9,8},{10,9},{11,1... | collective-permute-start | bytes 294920 | tf_op jit(solution)/shard_map/ppermute | solution.py:22
  227.2 7.7 %collective-permute-start.14 = (f32[3,16,4,128]{3,2,1,0:T(4,128)S(1)}, f32[3,16,4,128]{3,2,1,0:T(4,128)S(1)}, u32[]{:S(2)}, u32[]{:S(2)}) collective-permute-start(f32[3,16,4,128]{3,2,1,0:T(4,128)S(1)} %get-tuple-element.94), channel_id=1, source_target_pairs={{0,1},{1,2},{2,3},{3,4},{4,5},{5,6},{6,7},{7,8},{8,9},{9,10},{10,1... | collective-permute-start | bytes 294920 | tf_op jit(solution)/shard_map/ppermute | solution.py:19
  232.0 8.6 %collective-permute-start.15 = (f32[3,16,4,128]{3,2,1,0:T(4,128)S(1)}, f32[3,16,4,128]{3,2,1,0:T(4,128)S(1)}, u32[]{:S(2)}, u32[]{:S(2)}) collective-permute-start(f32[3,16,4,128]{3,2,1,0:T(4,128)S(1)} %get-tuple-element.95), channel_id=1, source_target_pairs={{1,0},{2,1},{3,2},{4,3},{5,4},{6,5},{7,6},{8,7},{9,8},{10,9},{11,1... | collective-permute-start | bytes 294920 | tf_op jit(solution)/shard_map/ppermute | solution.py:22
  241.3 1.1 copy-start.19
  241.3 1.1 copy-start.20
  241.3 1.1 copy-start.21
  (13 other events, 12.0 us)
where the time goes:
time: 248 us; the launch traced here: 247 us
  starting transfers between devices  155 us (62%)
  other arithmetic  67 us (27%)
  waiting for transfers between devices  11.9 us (5%)
  local copies, waits for them, and re-layouts  10.1 us (4%)
  between operations  2.5 us (1%)
    ppermute x16, starting transfers between devices, with_halo(): lax.ppermute(lax.slice_in_dim(block, 0, width, axis=dim), axis, backward)  94.4 us
    ppermute x16, starting transfers between devices, with_halo(): lax.ppermute(lax.slice_in_dim(block, block.shape[dim] - width, None, axis...  61.1 us
    scatter-add x5, other arithmetic, inject(): return field.at[jnp.clip(local_x, 0, cells_x - 1), jnp.clip(local_y, 0, c...  33.5 us
    ppermute x16, waiting for transfers between devices, with_halo(): lax.ppermute(lax.slice_in_dim(block, 0, width, axis=dim), axis, backward)  10.9 us
    concatenate x8, other arithmetic, with_halo(): block = jnp.concatenate([low, block, high], axis=dim)  7.72 us
    add x1, other arithmetic, imaging(): grads[2]  6.51 us
    unnamed x7, other arithmetic  6.46 us
  transfers between devices with their start and end apart: 32, of which 4 were waited for; matrix products, arithmetic and copies ran while one was open for 18% of the time, Pallas kernels for 0%

commit v1 on v0

v1 whole, which is shorter than its diff:
```python
import jax
import jax.numpy as jnp
from jax import lax
from jax.experimental import pallas as pl
from jax.experimental.pallas import tpu as pltpu
from jax.sharding import PartitionSpec as P

REC_DEPTH = 6
COEFS = (1225.0 / 1024.0, -245.0 / 3072.0, 49.0 / 5120.0, -5.0 / 7168.0)
TIME_STEP = 0.2
DAMPING = 0.3
MESH = pl.DeviceIdType.MESH

FS0, FV1, FS1, FV2, AS0, AV1, AS1, AV0 = range(8)
VELOCITY = (FV1, FV2, AV1, AV0)
UP, DOWN = 0, 1


def layers(e, way, c):
    backward = (c == 0) if e in VELOCITY else (c != 0)
    return 4 if backward == (way == UP) else 3


def diff(load, forward):
    total = None
    for order, coef in enumerate(COEFS, 1):
        high, low = (order, 1 - order) if forward else (order - 1, -order)
        term = coef * (load(high) - load(low))
        total = term if total is None else total + term
    return total


def kernel(
    fwd, adj, lam_in, mu_in, buo_in, src_x, src_y, src_z, src_w, width_in, rec_x, rec_y, residual,
    g_lam, g_mu, g_rho,
    px, py, ys, yr, szz, vel0, lam, mu, buo, damp, src, rinj, rates1,
    load_sem, xs_sem, xr_sem, ys_sem, yr_sem,
):
    gx, gy = lax.axis_index("gx"), lax.axis_index("gy")
    nx, ny = lax.axis_size("gx"), lax.axis_size("gy")
    cells_x, cells_y, depth = buo.shape
    pairs = cells_x // 2
    anchor_x, anchor_y = gx * cells_x, gy * cells_y
    total_x, total_y = nx * cells_x, ny * cells_y
    has = {("gx", UP): gx < nx - 1, ("gx", DOWN): gx > 0, ("gy", UP): gy < ny - 1, ("gy", DOWN): gy > 0}
    place = {"gx": gx, "gy": gy}

    def neighbour(axis, way):
        return {axis: place[axis] + (1 if way == UP else -1)}

    loads = {}

    def load(name, source, target):
        copy = pltpu.make_async_copy(source, target, load_sem.at[len(loads)])
        copy.start()
        loads[name] = copy

    middle, rows = pl.ds(4, cells_x), pl.ds(8, cells_y)
    for chain, (state, e) in enumerate(((fwd, FS0), (adj, AS0))):
        for c, k in enumerate((3, 6, 7)):
            load(("px", e, c), state.at[k], px.at[e, c, middle])
        for c, k in enumerate((4, 6, 8)):
            load(("py", e, c), state.at[k], py.at[e, c, :, rows])
    for chain, (state, e) in enumerate(((fwd, FS0), (adj, AS0))):
        load(("szz", e), state.at[5], szz.at[e])
        load(("vel", e), state.at[pl.ds(0, 3)], vel0.at[chain])
    load("buo", buo_in, buo)
    load("lam", lam_in, lam)
    load("mu", mu_in, mu)

    barrier = pltpu.get_barrier_semaphore()
    for (axis, way), there in has.items():
        @pl.when(there)
        def _(axis=axis, way=way):
            pl.semaphore_signal(barrier, inc=1, device_id=neighbour(axis, way), device_id_type=MESH)

    row = lax.broadcasted_iota(jnp.int32, (cells_y, depth), 0)
    lane = lax.broadcasted_iota(jnp.int32, (cells_y, depth), 1)
    width = width_in[0].astype(jnp.float32)

    def taper(dist):
        frac = jnp.maximum(width - dist.astype(jnp.float32), 0.0) / width
        return jnp.exp(-DAMPING * frac * frac)

    coord_y = anchor_y + row
    taper_y = taper(jnp.minimum(coord_y, total_y - 1 - coord_y))
    taper_z = taper(depth - 1 - lane)
    rec_row = anchor_y + lax.broadcasted_iota(jnp.int32, (cells_y, rec_x.shape[1]), 0) == rec_y[...]

    def prepare(p, carry):
        coord_x = jnp.zeros((cells_y, depth), jnp.int32) + (anchor_x + p)
        damp[p] = taper(jnp.minimum(coord_x, total_x - 1 - coord_x)) * taper_y * taper_z
        total = jnp.zeros((cells_y, depth), jnp.float32)
        for s in range(src_x.shape[0]):
            amount = jnp.where(src_x[s] == anchor_x + p, TIME_STEP * src_w[s], 0.0)
            hit = (coord_y == src_y[s]) & (lane == src_z[s])
            total = total + jnp.where(hit, amount, 0.0)
        src[p] = total
        for t in range(2):
            amounts = jnp.where(rec_x[...] == anchor_x + p, TIME_STEP * residual[pl.ds(t, 1), :], 0.0)
            column = jnp.sum(jnp.where(rec_row, amounts, 0.0), axis=1, keepdims=True)
            rinj[t, p] = jnp.where(lane == REC_DEPTH, column, 0.0)
        return carry

    lax.fori_loop(0, cells_x, prepare, 0)

    for way in (UP, DOWN):
        @pl.when(jnp.logical_not(has["gx", 1 - way]))
        def _(way=way):
            def fill(e, carry):
                px[e, :, pl.ds(0 if way == UP else 4 + cells_x, 4)] = jnp.zeros((3, 4, cells_y, depth), jnp.float32)
                return carry
            lax.fori_loop(0, 8, fill, 0)

        @pl.when(jnp.logical_not(has["gy", 1 - way]))
        def _(way=way):
            def fill(e, carry):
                yr[e, way] = jnp.zeros(yr.shape[2:], jnp.float32)
                return carry
            lax.fori_loop(0, 8, fill, 0)

    def x_copy(e, way, c, peer):
        n = layers(e, way, c)
        if way == UP:
            source, target = pl.ds(4 + cells_x - n, n), pl.ds(4 - n, n)
        else:
            source, target = pl.ds(4, n), pl.ds(4 + cells_x, n)
        return pltpu.make_async_remote_copy(
            px.at[e, c, source], px.at[e, c, target], xs_sem.at[e, way, c], xr_sem.at[e, way, c],
            device_id=neighbour("gx", peer), device_id_type=MESH,
        )

    def y_copy(e, way, peer):
        return pltpu.make_async_remote_copy(
            ys.at[e, way], yr.at[e, way], ys_sem.at[e, way], yr_sem.at[e, way],
            device_id=neighbour("gy", peer), device_id_type=MESH,
        )

    def send(e):
        for way in (UP, DOWN):
            @pl.when(has["gx", way])
            def _(way=way):
                for c in range(3):
                    x_copy(e, way, c, way).start()
        for way in (UP, DOWN):
            @pl.when(has["gy", way])
            def _(way=way):
                y_copy(e, way, way).start()

    def slot(c, p, odd):
        if c < 2:
            return p, pl.ds(4 * c, 4)
        return cells_x + p // 2, pl.ds(4 * odd, 4)

    def receive(e):
        for way in (UP, DOWN):
            @pl.when(has["gy", 1 - way])
            def _(way=way):
                y_copy(e, way, 1 - way).wait_recv()

        def unpack(q, carry):
            for odd in range(2):
                p = 2 * q + odd
                for c in range(3):
                    tile, part = slot(c, p, odd) if c < 2 else (cells_x + q, pl.ds(4 * odd, 4))
                    py[e, c, p, pl.ds(4, 4), :] = yr[e, UP, tile, part, :]
                    py[e, c, p, pl.ds(8 + cells_y, 4), :] = yr[e, DOWN, tile, part, :]
            return carry

        lax.fori_loop(0, pairs, unpack, 0)
        for way in (UP, DOWN):
            @pl.when(has["gx", 1 - way])
            def _(way=way):
                for c in range(3):
                    x_copy(e, way, c, 1 - way).wait_recv()

    def pack(e, c, q, odd, value):
        tile, part = (2 * q + odd, pl.ds(4 * c, 4)) if c < 2 else (cells_x + q, pl.ds(4 * odd, 4))
        ys[e, UP, tile, part, :] = value[cells_y - 4:]
        ys[e, DOWN, tile, part, :] = value[:4]

    def store_y(e, c, q, odd, value):
        py[e, c, 2 * q + odd, rows, :] = value
        pack(e, c, q, odd, value)

    def by_plane(body):
        def step(q, carry):
            for odd in range(2):
                body(q, odd, 2 * q + odd)
            return carry
        lax.fori_loop(0, pairs, step, 0)

    def diff_x(e, c, p, forward):
        return diff(lambda k: px[e, c, p + (4 + k)], forward)

    def diff_y(e, c, p, forward):
        return diff(lambda k: py[e, c, p, pl.ds(8 + k, cells_y), :], forward)

    def diff_z(value, forward):
        def at(k):
            if k == 0:
                return value
            moved = pltpu.roll(value, (-k) % depth, 1)
            return jnp.where(lane < depth - k if k > 0 else lane >= -k, moved, 0.0)
        return diff(at, forward)

    def center_x(e, c, p):
        return px[e, c, p + 4]

    def center_y(e, c, p):
        return py[e, c, p, rows, :]

    def stresses(e, p):
        return (
            center_x(e, 0, p), center_y(e, 0, p), szz[e, p],
            center_x(e, 1, p), center_x(e, 2, p), center_y(e, 2, p),
        )

    def velocity_half(e, target, before):
        def body(q, odd, p):
            s = stresses(e, p)
            force = (
                diff_x(e, 0, p, True) + diff_y(e, 1, p, False) + diff_z(s[4], False),
                diff_x(e, 1, p, False) + diff_y(e, 0, p, True) + diff_z(s[5], False),
                diff_x(e, 2, p, False) + diff_y(e, 2, p, False) + diff_z(s[2], True),
            )
            scaled = TIME_STEP * buo[p]
            for c in range(3):
                value = damp[p] * (before(c, p) + scaled * force[c])
                px[target, c, p + 4] = value
                store_y(target, c, q, odd, value)
        by_plane(body)

    def strain(e, p):
        vx, vy, vz = (center_x(e, c, p) for c in range(3))
        return (
            diff_x(e, 0, p, False),
            diff_y(e, 1, p, False),
            diff_z(vz, False),
            diff_y(e, 0, p, True) + diff_x(e, 1, p, True),
            diff_z(vx, True) + diff_x(e, 2, p, True),
            diff_z(vy, True) + diff_y(e, 2, p, True),
        )

    def stress_half(e, rates, p):
        s = stresses(e, p)
        normal = lam[p] * (rates[0] + rates[1] + rates[2])
        shear = TIME_STEP * mu[p]
        return [
            damp[p] * (s[k] + (TIME_STEP * normal + 2.0 * shear * rates[k])) for k in range(3)
        ] + [damp[p] * (s[k] + shear * rates[k]) for k in range(3, 6)]

    def store_stress(e, q, odd, p, s):
        for c, k in enumerate((0, 3, 4)):
            px[e, c, p + 4] = s[k]
        for c, k in enumerate((1, 3, 5)):
            store_y(e, c, q, odd, s[k])
        szz[e, p] = s[2]

    for e in (FS0, AS0):
        for c in range(3):
            loads["py", e, c].wait()

        def first(q, odd, p, e=e):
            for c in range(3):
                pack(e, c, q, odd, center_y(e, c, p))
        by_plane(first)
        for c in range(3):
            loads["px", e, c].wait()

    pl.semaphore_wait(barrier, sum(there.astype(jnp.int32) for there in has.values()))

    send(FS0)
    send(AS0)
    for name, copy in loads.items():
        if name[0] not in ("px", "py"):
            copy.wait()

    receive(FS0)
    velocity_half(FS0, FV1, lambda c, p: vel0[0, c, p])
    send(FV1)
    receive(AS0)
    velocity_half(AS0, AV1, lambda c, p: vel0[1, c, p])
    send(AV1)

    receive(FV1)

    def forward_stress(q, odd, p):
        rates = strain(FV1, p)
        for k in range(6):
            rates1[k, p] = rates[k]
        s = stress_half(FS0, rates, p)
        for k in range(3):
            s[k] = s[k] + src[p]
        store_stress(FS1, q, odd, p, s)
    by_plane(forward_stress)
    send(FS1)

    receive(AV1)

    def adjoint_stress(q, odd, p):
        store_stress(AS1, q, odd, p, stress_half(AS0, strain(AV1, p), p))
    by_plane(adjoint_stress)
    send(AS1)

    receive(FS1)
    velocity_half(FS1, FV2, lambda c, p: center_x(FV1, c, p))
    send(FV2)

    def adjoint_velocity(e, t, c, p):
        value = center_x(e, c, p)
        return value + rinj[t, p] if c == 2 else value

    receive(AS1)
    velocity_half(AS1, AV0, lambda c, p: adjoint_velocity(AV1, 0, c, p))
    send(AV0)

    def density(q, odd, p):
        total = None
        for c in range(3):
            one = center_x(FV1, c, p)
            term = (
                adjoint_velocity(AV1, 0, c, p) * (center_x(FV2, c, p) - one)
                + adjoint_velocity(AV0, 1, c, p) * (one - vel0[0, c, p])
            )
            total = term if total is None else total + term
        g_rho[p] = total / TIME_STEP
    by_plane(density)

    def image(rates, s):
        lam_term = (rates[0] + rates[1] + rates[2]) * (s[0] + s[1] + s[2])
        normal = rates[0] * s[0] + rates[1] * s[1] + rates[2] * s[2]
        return lam_term, 2.0 * normal + rates[3] * s[3] + rates[4] * s[4] + rates[5] * s[5]

    receive(FV2)

    def image_one(q, odd, p):
        g_lam[p], g_mu[p] = image(strain(FV2, p), stresses(AS1, p))
    by_plane(image_one)

    receive(AV0)

    def image_two(q, odd, p):
        s = stress_half(AS1, strain(AV0, p), p)
        lam_term, mu_term = image([rates1[k, p] for k in range(6)], s)
        g_lam[p] = g_lam[p] + lam_term
        g_mu[p] = g_mu[p] + mu_term
    by_plane(image_two)

    for e in range(8):
        for way in (UP, DOWN):
            @pl.when(has["gx", way])
            def _(e=e, way=way):
                for c in range(3):
                    x_copy(e, way, c, way).wait_send()

            @pl.when(has["gy", way])
            def _(e=e, way=way):
                y_copy(e, way, way).wait_send()


def local(
    forward_state, adjoint_state, lame_lambda, lame_mu, buoyancy,
    source_x, source_y, source_z, source_wavelet,
    receiver_x, receiver_y, receiver_residual, absorb_width,
):
    block = buoyancy.shape
    cells_x, cells_y, depth = block
    f32 = jnp.float32
    hbm, vmem, smem = (pl.BlockSpec(memory_space=m) for m in (pl.ANY, pltpu.VMEM, pltpu.SMEM))
    dma = pltpu.SemaphoreType.DMA
    packed = (8, 2, cells_x + cells_x // 2, 8, depth)
    return pl.pallas_call(
        kernel,
        out_shape=[jax.ShapeDtypeStruct(block, f32)] * 3,
        in_specs=[hbm] * 5 + [smem] * 5 + [vmem] * 3,
        out_specs=[vmem] * 3,
        scratch_shapes=[
            pltpu.VMEM((8, 3, cells_x + 8, cells_y, depth), f32),
            pltpu.VMEM((8, 3, cells_x, cells_y + 16, depth), f32),
            pltpu.VMEM(packed, f32),
            pltpu.VMEM(packed, f32),
            pltpu.VMEM((8,) + block, f32),
            pltpu.VMEM((2, 3) + block, f32),
            pltpu.VMEM(block, f32),
            pltpu.VMEM(block, f32),
            pltpu.VMEM(block, f32),
            pltpu.VMEM(block, f32),
            pltpu.VMEM(block, f32),
            pltpu.VMEM((2,) + block, f32),
            pltpu.VMEM((6,) + block, f32),
            dma((19,)),
            dma((8, 2, 3)),
            dma((8, 2, 3)),
            dma((8, 2)),
            dma((8, 2)),
        ],
        compiler_params=pltpu.CompilerParams(
            collective_id=0, has_side_effects=True, vmem_limit_bytes=60 * 1024 * 1024
        ),
        name="window",
    )(
        forward_state, adjoint_state, lame_lambda, lame_mu, buoyancy,
        source_x, source_y, source_z, source_wavelet, absorb_width,
        receiver_x.reshape(1, -1), receiver_y.reshape(1, -1), receiver_residual,
    )


def solution(mesh):
    volume = P("gx", "gy", None)
    state = P(None, "gx", "gy", None)
    return jax.shard_map(
        local,
        mesh=mesh,
        in_specs=(state, state, volume, volume, volume) + (P(),) * 8,
        out_specs=(volume, volume, volume),
        check_vma=False,
    )
```

time: 248 us -> 56.4 us (0.23)
  the two profiles are of different devices: /device:TPU:270 before, /device:TPU:393 now
where the time goes in v1:
time: 56.4 us; the launch traced here: 56.2 us
  Pallas kernels  51.9 us (92%)
  local copies, waits for them, and re-layouts  3 us (5%)
  between operations  1.3 us (2%)
    pallas_call x1, Pallas kernels, local(): pl.pallas_call(kernel, out_shape=[jax.ShapeDtypeStruct(block, f32)] * 3,...  51.9 us
    unnamed x7, local copies, waits for them, and re-layouts  3 us

profile of v1, /device:TPU:393, one launch (start us, length us, event | category | flops | bytes accessed | tf_op | source)
XLA Modules:
  0.0 56.2 jit_solution(9126858534759003534)
XLA Ops:
  1.3 51.9 %window.1 = (f32[8,16,128]{2,1,0:T(8,128)}, f32[8,16,128]{2,1,0:T(8,128)}, f32[8,16,128]{2,1,0:T(8,128)}) custom-call(f32[9,8,16,128]{3,2,1,0:T(8,128)} %fwd.1, f32[9,8,16,128]{3,2,1,0:T(8,128)} %adj.1, f32[8,16,128]{2,1,0:T(8,128)} %lam_in.1, f32[8,16,128]{2,1,0:T(8,128)} %mu_in.1, f32[8,16,128]{2,1,0:T(8,128)} %buo_in.1, s32[8]{0:T(128)} %src_x.1, ...), custom_call_target="tpu_custom_call" | custom-call | tf_op jit(solution)/shard_map/window/pallas_call | solution.py:373
  53.1 0.0 copy-start.1
  53.2 1.5 %copy.20 = f32[8,16,128]{2,1,0:T(8,128)} copy(f32[8,16,128]{2,1,0:T(8,128)} %get-tuple-element.6) | data formatting | bytes 131072
  54.7 0.0 copy-done.1
  54.7 0.0 copy-start
  54.7 0.6 %copy.21 = f32[8,16,128]{2,1,0:T(8,128)} copy(f32[8,16,128]{2,1,0:T(8,128)S(1)} %copy-done.1) | data formatting | bytes 131072
  55.3 0.2 copy-done
  55.5 0.6 %copy.22 = f32[8,16,128]{2,1,0:T(8,128)} copy(f32[8,16,128]{2,1,0:T(8,128)S(1)} %copy-done) | data formatting | bytes 131072
Async XLA Ops:
  53.1 1.5 %copy-start.1 = (f32[8,16,128]{2,1,0:T(8,128)S(1)}, f32[8,16,128]{2,1,0:T(8,128)}, u32[]{:S(2)}) copy-start(f32[8,16,128]{2,1,0:T(8,128)} %get-tuple-element.7) | copy-start | bytes 196612
  54.7 0.9 %copy-start = (f32[8,16,128]{2,1,0:T(8,128)S(1)}, f32[8,16,128]{2,1,0:T(8,128)}, u32[]{:S(2)}) copy-start(f32[8,16,128]{2,1,0:T(8,128)} %get-tuple-element.8) | copy-start | bytes 196612

commit v2 on v1

--- a/solution.py
+++ b/solution.py
@@ -76,48 +76,58 @@
 
     row = lax.broadcasted_iota(jnp.int32, (cells_y, depth), 0)
     lane = lax.broadcasted_iota(jnp.int32, (cells_y, depth), 1)
-    width = width_in[0].astype(jnp.float32)
-
-    def taper(dist):
-        frac = jnp.maximum(width - dist.astype(jnp.float32), 0.0) / width
-        return jnp.exp(-DAMPING * frac * frac)
-
     coord_y = anchor_y + row
-    taper_y = taper(jnp.minimum(coord_y, total_y - 1 - coord_y))
-    taper_z = taper(depth - 1 - lane)
-    rec_row = anchor_y + lax.broadcasted_iota(jnp.int32, (cells_y, rec_x.shape[1]), 0) == rec_y[...]
-
-    def prepare(p, carry):
-        coord_x = jnp.zeros((cells_y, depth), jnp.int32) + (anchor_x + p)
-        damp[p] = taper(jnp.minimum(coord_x, total_x - 1 - coord_x)) * taper_y * taper_z
-        total = jnp.zeros((cells_y, depth), jnp.float32)
-        for s in range(src_x.shape[0]):
-            amount = jnp.where(src_x[s] == anchor_x + p, TIME_STEP * src_w[s], 0.0)
-            hit = (coord_y == src_y[s]) & (lane == src_z[s])
-            total = total + jnp.where(hit, amount, 0.0)
-        src[p] = total
-        for t in range(2):
-            amounts = jnp.where(rec_x[...] == anchor_x + p, TIME_STEP * residual[pl.ds(t, 1), :], 0.0)
-            column = jnp.sum(jnp.where(rec_row, amounts, 0.0), axis=1, keepdims=True)
-            rinj[t, p] = jnp.where(lane == REC_DEPTH, column, 0.0)
-        return carry
-
-    lax.fori_loop(0, cells_x, prepare, 0)
-
-    for way in (UP, DOWN):
-        @pl.when(jnp.logical_not(has["gx", 1 - way]))
-        def _(way=way):
-            def fill(e, carry):
-                px[e, :, pl.ds(0 if way == UP else 4 + cells_x, 4)] = jnp.zeros((3, 4, cells_y, depth), jnp.float32)
-                return carry
-            lax.fori_loop(0, 8, fill, 0)
-
-        @pl.when(jnp.logical_not(has["gy", 1 - way]))
-        def _(way=way):
-            def fill(e, carry):
-                yr[e, way] = jnp.zeros(yr.shape[2:], jnp.float32)
-                return carry
-            lax.fori_loop(0, 8, fill, 0)
+
+    def set_damping():
+        width = width_in[0].astype(jnp.float32)
+
+        def taper(dist):
+            frac = jnp.maximum(width - dist.astype(jnp.float32), 0.0) / width
+            return jnp.exp(-DAMPING * frac * frac)
+
+        taper_y = taper(jnp.minimum(coord_y, total_y - 1 - coord_y))
+        taper_z = taper(depth - 1 - lane)
+
+        def plane(p, carry):
+            coord_x = jnp.zeros((cells_y, depth), jnp.int32) + (anchor_x + p)
+            damp[p] = taper(jnp.minimum(coord_x, total_x - 1 - coord_x)) * taper_y * taper_z
+            return carry
+
+        lax.fori_loop(0, cells_x, plane, 0)
+
+    def set_injections():
+        rec_row = anchor_y + lax.broadcasted_iota(jnp.int32, (cells_y, rec_x.shape[1]), 0) == rec_y[...]
+
+        def plane(p, carry):
+            total = jnp.zeros((cells_y, depth), jnp.float32)
+            for s in range(src_x.shape[0]):
+                amount = jnp.where(src_x[s] == anchor_x + p, TIME_STEP * src_w[s], 0.0)
+                hit = (coord_y == src_y[s]) & (lane == src_z[s])
+                total = total + jnp.where(hit, amount, 0.0)
+            src[p] = total
+            for t in range(2):
+                amounts = jnp.where(rec_x[...] == anchor_x + p, TIME_STEP * residual[pl.ds(t, 1), :], 0.0)
+                column = jnp.sum(jnp.where(rec_row, amounts, 0.0), axis=1, keepdims=True)
+                rinj[t, p] = jnp.where(lane == REC_DEPTH, column, 0.0)
+            return carry
+
+        lax.fori_loop(0, cells_x, plane, 0)
+
+    def set_zeros():
+        for way in (UP, DOWN):
+            @pl.when(jnp.logical_not(has["gx", 1 - way]))
+            def _(way=way):
+                def fill(e, carry):
+                    px[e, :, pl.ds(0 if way == UP else 4 + cells_x, 4)] = jnp.zeros((3, 4, cells_y, depth), jnp.float32)
+                    return carry
+                lax.fori_loop(0, 8, fill, 0)
+
+            @pl.when(jnp.logical_not(has["gy", 1 - way]))
+            def _(way=way):
+                def fill(e, carry):
+                    yr[e, way] = jnp.zeros(yr.shape[2:], jnp.float32)
+                    return carry
+                lax.fori_loop(0, 8, fill, 0)
 
     def x_copy(e, way, c, peer):
         n = layers(e, way, c)
@@ -136,46 +146,66 @@
             device_id=neighbour("gy", peer), device_id_type=MESH,
         )
 
-    def send(e):
-        for way in (UP, DOWN):
-            @pl.when(has["gx", way])
+    odd_block = lax.rem(gx, 2)
+    is_near = {UP: odd_block == 0, DOWN: odd_block == 1}
+
+    def x_side(near, way):
+        there = is_near[way] if near else jnp.logical_not(is_near[way])
+        return jnp.logical_and(there, has["gx", way])
+
+    def send_x(e, near):
+        for way in (UP, DOWN):
+            @pl.when(x_side(near, way))
             def _(way=way):
                 for c in range(3):
                     x_copy(e, way, c, way).start()
-        for way in (UP, DOWN):
-            @pl.when(has["gy", way])
-            def _(way=way):
-                y_copy(e, way, way).start()
-
-    def slot(c, p, odd):
-        if c < 2:
-            return p, pl.ds(4 * c, 4)
-        return cells_x + p // 2, pl.ds(4 * odd, 4)
-
-    def receive(e):
-        for way in (UP, DOWN):
-            @pl.when(has["gy", 1 - way])
-            def _(way=way):
-                y_copy(e, way, 1 - way).wait_recv()
-
-        def unpack(q, carry):
-            for odd in range(2):
-                p = 2 * q + odd
+
+    def sent_x(e, near):
+        for way in (UP, DOWN):
+            @pl.when(x_side(near, way))
+            def _(way=way):
                 for c in range(3):
-                    tile, part = slot(c, p, odd) if c < 2 else (cells_x + q, pl.ds(4 * odd, 4))
-                    py[e, c, p, pl.ds(4, 4), :] = yr[e, UP, tile, part, :]
-                    py[e, c, p, pl.ds(8 + cells_y, 4), :] = yr[e, DOWN, tile, part, :]
-            return carry
-
-        lax.fori_loop(0, pairs, unpack, 0)
-        for way in (UP, DOWN):
-            @pl.when(has["gx", 1 - way])
+                    x_copy(e, way, c, way).wait_send()
+
+    def receive_x(e, near):
+        for way in (UP, DOWN):
+            @pl.when(x_side(near, 1 - way))
             def _(way=way):
                 for c in range(3):
                     x_copy(e, way, c, 1 - way).wait_recv()
 
+    def send_y(e):
+        for way in (UP, DOWN):
+            @pl.when(has["gy", way])
+            def _(way=way):
+                y_copy(e, way, way).start()
+
+    def sent_y(e):
+        for way in (UP, DOWN):
+            @pl.when(has["gy", way])
+            def _(way=way):
+                y_copy(e, way, way).wait_send()
+
+    def receive_y(e):
+        for way in (UP, DOWN):
+            @pl.when(has["gy", 1 - way])
+            def _(way=way):
+                y_copy(e, way, 1 - way).wait_recv()
+
+        def unpack(q, odd, p):
+            for c in range(3):
+                tile, part = slot(c, q, odd)
+                py[e, c, p, pl.ds(4, 4), :] = yr[e, UP, tile, part, :]
+                py[e, c, p, pl.ds(8 + cells_y, 4), :] = yr[e, DOWN, tile, part, :]
+        by_plane(unpack)
+
+    def slot(c, q, odd):
+        if c < 2:
+            return 2 * q + odd, pl.ds(4 * c, 4)
+        return cells_x + q, pl.ds(4 * odd, 4)
+
     def pack(e, c, q, odd, value):
-        tile, part = (2 * q + odd, pl.ds(4 * c, 4)) if c < 2 else (cells_x + q, pl.ds(4 * odd, 4))
+        tile, part = slot(c, q, odd)
         ys[e, UP, tile, part, :] = value[cells_y - 4:]
         ys[e, DOWN, tile, part, :] = value[:4]
 
@@ -183,12 +213,30 @@
         py[e, c, 2 * q + odd, rows, :] = value
         pack(e, c, q, odd, value)
 
-    def by_plane(body):
-        def step(q, carry):
+    def by_plane(body, first=0, count=pairs):
+        def step(i, carry):
+            q = first + i
             for odd in range(2):
                 body(q, odd, 2 * q + odd)
             return carry
-        lax.fori_loop(0, pairs, step, 0)
+        lax.fori_loop(0, count, step, 0)
+
+    half = pairs // 2
+    first_pair = {True: half * (1 - odd_block), False: half * odd_block}
+
+    def near_half(e, body, target=None):
+        receive_y(e)
+        receive_x(e, True)
+        by_plane(body, first_pair[True], half)
+        if target is not None:
+            send_x(target, True)
+
+    def far_half(e, body, target=None):
+        receive_x(e, False)
+        by_plane(body, first_pair[False], half)
+        if target is not None:
+            send_x(target, False)
+            send_y(target)
 
     def diff_x(e, c, p, forward):
         return diff(lambda k: px[e, c, p + (4 + k)], forward)
@@ -229,7 +277,7 @@
                 value = damp[p] * (before(c, p) + scaled * force[c])
                 px[target, c, p + 4] = value
                 store_y(target, c, q, odd, value)
-        by_plane(body)
+        return body
 
     def strain(e, p):
         vx, vy, vz = (center_x(e, c, p) for c in range(3))
@@ -257,34 +305,6 @@
             store_y(e, c, q, odd, s[k])
         szz[e, p] = s[2]
 
-    for e in (FS0, AS0):
-        for c in range(3):
-            loads["py", e, c].wait()
-
-        def first(q, odd, p, e=e):
-            for c in range(3):
-                pack(e, c, q, odd, center_y(e, c, p))
-        by_plane(first)
-        for c in range(3):
-            loads["px", e, c].wait()
-
-    pl.semaphore_wait(barrier, sum(there.astype(jnp.int32) for there in has.values()))
-
-    send(FS0)
-    send(AS0)
-    for name, copy in loads.items():
-        if name[0] not in ("px", "py"):
-            copy.wait()
-
-    receive(FS0)
-    velocity_half(FS0, FV1, lambda c, p: vel0[0, c, p])
-    send(FV1)
-    receive(AS0)
-    velocity_half(AS0, AV1, lambda c, p: vel0[1, c, p])
-    send(AV1)
-
-    receive(FV1)
-
     def forward_stress(q, odd, p):
         rates = strain(FV1, p)
         for k in range(6):
@@ -293,27 +313,13 @@
         for k in range(3):
             s[k] = s[k] + src[p]
         store_stress(FS1, q, odd, p, s)
-    by_plane(forward_stress)
-    send(FS1)
-
-    receive(AV1)
 
     def adjoint_stress(q, odd, p):
         store_stress(AS1, q, odd, p, stress_half(AS0, strain(AV1, p), p))
-    by_plane(adjoint_stress)
-    send(AS1)
-
-    receive(FS1)
-    velocity_half(FS1, FV2, lambda c, p: center_x(FV1, c, p))
-    send(FV2)
 
     def adjoint_velocity(e, t, c, p):
         value = center_x(e, c, p)
         return value + rinj[t, p] if c == 2 else value
-
-    receive(AS1)
-    velocity_half(AS1, AV0, lambda c, p: adjoint_velocity(AV1, 0, c, p))
-    send(AV0)
 
     def density(q, odd, p):
         total = None
@@ -325,38 +331,91 @@
             )
             total = term if total is None else total + term
         g_rho[p] = total / TIME_STEP
-    by_plane(density)
 
     def image(rates, s):
         lam_term = (rates[0] + rates[1] + rates[2]) * (s[0] + s[1] + s[2])
         normal = rates[0] * s[0] + rates[1] * s[1] + rates[2] * s[2]
         return lam_term, 2.0 * normal + rates[3] * s[3] + rates[4] * s[4] + rates[5] * s[5]
 
-    receive(FV2)
-
     def image_one(q, odd, p):
         g_lam[p], g_mu[p] = image(strain(FV2, p), stresses(AS1, p))
-    by_plane(image_one)
-
-    receive(AV0)
 
     def image_two(q, odd, p):
         s = stress_half(AS1, strain(AV0, p), p)
         lam_term, mu_term = image([rates1[k, p] for k in range(6)], s)
         g_lam[p] = g_lam[p] + lam_term
         g_mu[p] = g_mu[p] + mu_term
-    by_plane(image_two)
+
+    forward_one = velocity_half(FS0, FV1, lambda c, p: vel0[0, c, p])
+    adjoint_one = velocity_half(AS0, AV1, lambda c, p: vel0[1, c, p])
+    forward_two = velocity_half(FS1, FV2, lambda c, p: center_x(FV1, c, p))
+    adjoint_two = velocity_half(AS1, AV0, lambda c, p: adjoint_velocity(AV1, 0, c, p))
+
+    def ready(e):
+        for c in range(3):
+            loads["py", e, c].wait()
+
+        def first(q, odd, p):
+            for c in range(3):
+                pack(e, c, q, odd, center_y(e, c, p))
+        by_plane(first)
+        for c in range(3):
+            loads["px", e, c].wait()
+
+    ready(FS0)
+    ready(AS0)
+    set_damping()
+    pl.semaphore_wait(barrier, sum(there.astype(jnp.int32) for there in has.values()))
+    for near in (False, True):
+        send_x(FS0, near)
+    send_y(FS0)
+    set_zeros()
+    set_injections()
+    for name, copy in loads.items():
+        if name[0] not in ("px", "py"):
+            copy.wait()
+
+    near_half(FS0, forward_one, FV1)
+    sent_x(FS0, False)
+    for near in (False, True):
+        send_x(AS0, near)
+    send_y(AS0)
+    near_half(AS0, adjoint_one, AV1)
+
+    far_half(FS0, forward_one, FV1)
+    near_half(FV1, forward_stress, FS1)
+    far_half(AS0, adjoint_one, AV1)
+    near_half(AV1, adjoint_stress, AS1)
+
+    far_half(FV1, forward_stress, FS1)
+    near_half(FS1, forward_two, FV2)
+    far_half(AV1, adjoint_stress, AS1)
+    near_half(AS1, adjoint_two, AV0)
+
+    far_half(FS1, forward_two, FV2)
+    near_half(FV2, image_one)
+    far_half(AS1, adjoint_two, AV0)
+    by_plane(density)
+    near_half(AV0, image_two)
+
+    far_half(FV2, image_one)
+    far_half(AV0, image_two)
 
     for e in range(8):
-        for way in (UP, DOWN):
-            @pl.when(has["gx", way])
-            def _(e=e, way=way):
-                for c in range(3):
-                    x_copy(e, way, c, way).wait_send()
-
-            @pl.when(has["gy", way])
-            def _(e=e, way=way):
-                y_copy(e, way, way).wait_send()
+        if e != FS0:
+            sent_x(e, False)
+        sent_x(e, True)
+        sent_y(e)
+
+
+def hand_on(*refs):
+    count = len(refs) // 2
+    sem = refs[-1]
+    copies = [pltpu.make_async_copy(refs[i], refs[count + i], sem.at[i]) for i in range(count)]
+    for copy in copies:
+        copy.start()
+    for copy in copies:
+        copy.wait()
 
 
 def local(
@@ -370,9 +429,10 @@
     hbm, vmem, smem = (pl.BlockSpec(memory_space=m) for m in (pl.ANY, pltpu.VMEM, pltpu.SMEM))
     dma = pltpu.SemaphoreType.DMA
     packed = (8, 2, cells_x + cells_x // 2, 8, depth)
-    return pl.pallas_call(
+    shapes = [jax.ShapeDtypeStruct(block, f32)] * 3
+    grads = pl.pallas_call(
         kernel,
-        out_shape=[jax.ShapeDtypeStruct(block, f32)] * 3,
+        out_shape=shapes,
         in_specs=[hbm] * 5 + [smem] * 5 + [vmem] * 3,
         out_specs=[vmem] * 3,
         scratch_shapes=[
@@ -404,6 +464,15 @@
         source_x, source_y, source_z, source_wavelet, absorb_width,
         receiver_x.reshape(1, -1), receiver_y.reshape(1, -1), receiver_residual,
     )
+    return pl.pallas_call(
+        hand_on,
+        out_shape=shapes,
+        in_specs=[hbm] * 3,
+        out_specs=[hbm] * 3,
+        scratch_shapes=[dma((3,))],
+        compiler_params=pltpu.CompilerParams(vmem_limit_bytes=60 * 1024 * 1024),
+        name="hand_on",
+    )(*grads)
 
 
 def solution(mesh):

time: 56.4 us -> 79.6 us (1.41)
  the two profiles are of different devices: /device:TPU:393 before, /device:TPU:326 now
where the time goes in v2:
time: 79.6 us; the launch traced here: 79.4 us
  Pallas kernels  78.2 us (98%)
  between operations  1.29 us (2%)
    pallas_call x1, Pallas kernels, local(): pl.pallas_call(kernel, out_shape=shapes, in_specs=[hbm] * 5 + [smem] * 5...  71.1 us
    pallas_call x1, Pallas kernels, local(): pl.pallas_call(hand_on, out_shape=shapes, in_specs=[hbm] * 3, out_specs=[...  7.09 us

profile of v2, /device:TPU:326, one launch (start us, length us, event | category | flops | bytes accessed | tf_op | source)
XLA Modules:
  0.0 79.4 jit_solution(3813609059655972591)
XLA Ops:
  1.3 71.1 %window.1 = (f32[8,16,128]{2,1,0:T(8,128)}, f32[8,16,128]{2,1,0:T(8,128)}, f32[8,16,128]{2,1,0:T(8,128)}) custom-call(f32[9,8,16,128]{3,2,1,0:T(8,128)} %fwd.1, f32[9,8,16,128]{3,2,1,0:T(8,128)} %adj.1, f32[8,16,128]{2,1,0:T(8,128)} %lam_in.1, f32[8,16,128]{2,1,0:T(8,128)} %mu_in.1, f32[8,16,128]{2,1,0:T(8,128)} %buo_in.1, s32[8]{0:T(128)} %src_x.1, ...), custom_call_target="tpu_custom_call" | custom-call | tf_op jit(solution)/shard_map/window/pallas_call | solution.py:433
  72.4 7.1 %hand_on.1 = (f32[8,16,128]{2,1,0:T(8,128)}, f32[8,16,128]{2,1,0:T(8,128)}, f32[8,16,128]{2,1,0:T(8,128)}) custom-call(f32[8,16,128]{2,1,0:T(8,128)} %get-tuple-element.6.refs_0_, f32[8,16,128]{2,1,0:T(8,128)} %get-tuple-element.7.refs_1_, f32[8,16,128]{2,1,0:T(8,128)} %get-tuple-element.8.refs_2_), custom_call_target="tpu_custom_call" | custom-call | tf_op jit(solution)/shard_map/hand_on/pallas_call | solution.py:467

commit v3 on v2

--- a/solution.py
+++ b/solution.py
@@ -213,27 +213,32 @@
         py[e, c, 2 * q + odd, rows, :] = value
         pack(e, c, q, odd, value)
 
-    def by_plane(body, first=0, count=pairs):
-        def step(i, carry):
-            q = first + i
+    def by_plane(body):
+        def step(q, carry):
             for odd in range(2):
                 body(q, odd, 2 * q + odd)
             return carry
-        lax.fori_loop(0, count, step, 0)
+        lax.fori_loop(0, pairs, step, 0)
 
     half = pairs // 2
-    first_pair = {True: half * (1 - odd_block), False: half * odd_block}
-
-    def near_half(e, body, target=None):
+
+    def stage(e, body, target=None):
         receive_y(e)
         receive_x(e, True)
-        by_plane(body, first_pair[True], half)
-        if target is not None:
-            send_x(target, True)
-
-    def far_half(e, body, target=None):
-        receive_x(e, False)
-        by_plane(body, first_pair[False], half)
+
+        def step(i, carry):
+            @pl.when(i == half)
+            def _():
+                if target is not None:
+                    send_x(target, True)
+                receive_x(e, False)
+
+            q = lax.rem(i + half * (1 - odd_block), pairs)
+            for odd in range(2):
+                body(q, odd, 2 * q + odd)
+            return carry
+
+        lax.fori_loop(0, pairs, step, 0)
         if target is not None:
             send_x(target, False)
             send_y(target)
@@ -366,56 +371,35 @@
     ready(AS0)
     set_damping()
     pl.semaphore_wait(barrier, sum(there.astype(jnp.int32) for there in has.values()))
-    for near in (False, True):
-        send_x(FS0, near)
-    send_y(FS0)
+    def send_first(e):
+        for near in (False, True):
+            send_x(e, near)
+        send_y(e)
+
+    send_first(FS0)
     set_zeros()
     set_injections()
     for name, copy in loads.items():
         if name[0] not in ("px", "py"):
             copy.wait()
-
-    near_half(FS0, forward_one, FV1)
     sent_x(FS0, False)
-    for near in (False, True):
-        send_x(AS0, near)
-    send_y(AS0)
-    near_half(AS0, adjoint_one, AV1)
-
-    far_half(FS0, forward_one, FV1)
-    near_half(FV1, forward_stress, FS1)
-    far_half(AS0, adjoint_one, AV1)
-    near_half(AV1, adjoint_stress, AS1)
-
-    far_half(FV1, forward_stress, FS1)
-    near_half(FS1, forward_two, FV2)
-    far_half(AV1, adjoint_stress, AS1)
-    near_half(AS1, adjoint_two, AV0)
-
-    far_half(FS1, forward_two, FV2)
-    near_half(FV2, image_one)
-    far_half(AS1, adjoint_two, AV0)
+    send_first(AS0)
+
+    stage(FS0, forward_one, FV1)
+    stage(AS0, adjoint_one, AV1)
+    stage(FV1, forward_stress, FS1)
+    stage(AV1, adjoint_stress, AS1)
+    stage(FS1, forward_two, FV2)
+    stage(AS1, adjoint_two, AV0)
     by_plane(density)
-    near_half(AV0, image_two)
-
-    far_half(FV2, image_one)
-    far_half(AV0, image_two)
+    stage(FV2, image_one)
+    stage(AV0, image_two)
 
     for e in range(8):
         if e != FS0:
             sent_x(e, False)
         sent_x(e, True)
         sent_y(e)
-
-
-def hand_on(*refs):
-    count = len(refs) // 2
-    sem = refs[-1]
-    copies = [pltpu.make_async_copy(refs[i], refs[count + i], sem.at[i]) for i in range(count)]
-    for copy in copies:
-        copy.start()
-    for copy in copies:
-        copy.wait()
 
 
 def local(
@@ -429,10 +413,9 @@
     hbm, vmem, smem = (pl.BlockSpec(memory_space=m) for m in (pl.ANY, pltpu.VMEM, pltpu.SMEM))
     dma = pltpu.SemaphoreType.DMA
     packed = (8, 2, cells_x + cells_x // 2, 8, depth)
-    shapes = [jax.ShapeDtypeStruct(block, f32)] * 3
-    grads = pl.pallas_call(
+    return pl.pallas_call(
         kernel,
-        out_shape=shapes,
+        out_shape=[jax.ShapeDtypeStruct(block, f32)] * 3,
         in_specs=[hbm] * 5 + [smem] * 5 + [vmem] * 3,
         out_specs=[vmem] * 3,
         scratch_shapes=[
@@ -464,15 +447,6 @@
         source_x, source_y, source_z, source_wavelet, absorb_width,
         receiver_x.reshape(1, -1), receiver_y.reshape(1, -1), receiver_residual,
     )
-    return pl.pallas_call(
-        hand_on,
-        out_shape=shapes,
-        in_specs=[hbm] * 3,
-        out_specs=[hbm] * 3,
-        scratch_shapes=[dma((3,))],
-        compiler_params=pltpu.CompilerParams(vmem_limit_bytes=60 * 1024 * 1024),
-        name="hand_on",
-    )(*grads)
 
 
 def solution(mesh):

time: 79.6 us -> 56.5 us (0.71)
  the two profiles are of different devices: /device:TPU:326 before, /device:TPU:393 now
where the time goes in v3:
time: 56.5 us; the launch traced here: 56.2 us
  Pallas kernels  51.9 us (92%)
  local copies, waits for them, and re-layouts  3 us (5%)
  between operations  1.3 us (2%)
    pallas_call x1, Pallas kernels, local(): pl.pallas_call(kernel, out_shape=[jax.ShapeDtypeStruct(block, f32)] * 3,...  51.9 us
    unnamed x7, local copies, waits for them, and re-layouts  3 us

profile of v3, /device:TPU:393, one launch (start us, length us, event | category | flops | bytes accessed | tf_op | source)
XLA Modules:
  0.0 56.2 jit_solution(8204905945212815911)
XLA Ops:
  1.3 51.9 %window.1 = (f32[8,16,128]{2,1,0:T(8,128)}, f32[8,16,128]{2,1,0:T(8,128)}, f32[8,16,128]{2,1,0:T(8,128)}) custom-call(f32[9,8,16,128]{3,2,1,0:T(8,128)} %fwd.1, f32[9,8,16,128]{3,2,1,0:T(8,128)} %adj.1, f32[8,16,128]{2,1,0:T(8,128)} %lam_in.1, f32[8,16,128]{2,1,0:T(8,128)} %mu_in.1, f32[8,16,128]{2,1,0:T(8,128)} %buo_in.1, s32[8]{0:T(128)} %src_x.1, ...), custom_call_target="tpu_custom_call" | custom-call | tf_op jit(solution)/shard_map/window/pallas_call | solution.py:416
  53.2 0.0 copy-start.1
  53.2 1.5 %copy.20 = f32[8,16,128]{2,1,0:T(8,128)} copy(f32[8,16,128]{2,1,0:T(8,128)} %get-tuple-element.6) | data formatting | bytes 131072
  54.7 0.0 copy-done.1
  54.7 0.0 copy-start
  54.7 0.6 %copy.21 = f32[8,16,128]{2,1,0:T(8,128)} copy(f32[8,16,128]{2,1,0:T(8,128)S(1)} %copy-done.1) | data formatting | bytes 131072
  55.3 0.2 copy-done
  55.5 0.6 %copy.22 = f32[8,16,128]{2,1,0:T(8,128)} copy(f32[8,16,128]{2,1,0:T(8,128)S(1)} %copy-done) | data formatting | bytes 131072
Async XLA Ops:
  53.2 1.5 %copy-start.1 = (f32[8,16,128]{2,1,0:T(8,128)S(1)}, f32[8,16,128]{2,1,0:T(8,128)}, u32[]{:S(2)}) copy-start(f32[8,16,128]{2,1,0:T(8,128)} %get-tuple-element.7) | copy-start | bytes 196612
  54.7 0.9 %copy-start = (f32[8,16,128]{2,1,0:T(8,128)S(1)}, f32[8,16,128]{2,1,0:T(8,128)}, u32[]{:S(2)}) copy-start(f32[8,16,128]{2,1,0:T(8,128)} %get-tuple-element.8) | copy-start | bytes 196612

commit v4 on v3

--- a/solution.py
+++ b/solution.py
@@ -14,6 +14,10 @@
 FS0, FV1, FS1, FV2, AS0, AV1, AS1, AV0 = range(8)
 VELOCITY = (FV1, FV2, AV1, AV0)
 UP, DOWN = 0, 1
+
+RUN = 4
+TO_RELAY = {(UP, 0): RUN, (UP, 1): 1 - RUN, (DOWN, 0): RUN - 1, (DOWN, 1): -RUN}
+FROM_RELAY = {(UP, 0): 1 - RUN, (UP, 1): RUN, (DOWN, 0): -RUN, (DOWN, 1): RUN - 1}
 
 
 def layers(e, way, c):
@@ -33,8 +37,8 @@
 def kernel(
     fwd, adj, lam_in, mu_in, buo_in, src_x, src_y, src_z, src_w, width_in, rec_x, rec_y, residual,
     g_lam, g_mu, g_rho,
-    px, py, ys, yr, szz, vel0, lam, mu, buo, damp, src, rinj, rates1,
-    load_sem, xs_sem, xr_sem, ys_sem, yr_sem,
+    px, py, ys, yr, relayed, szz, vel0, lam, mu, buo, damp, src, rinj, rates1,
+    load_sem, xs_sem, xr_sem, ys_sem, yr_sem, hop_sem, forward_sem,
 ):
     gx, gy = lax.axis_index("gx"), lax.axis_index("gy")
     nx, ny = lax.axis_size("gx"), lax.axis_size("gy")
@@ -47,6 +51,30 @@
 
     def neighbour(axis, way):
         return {axis: place[axis] + (1 if way == UP else -1)}
+
+    column, wraps = lax.rem(gy, RUN), ny > RUN
+    at_end = {UP: column == RUN - 1, DOWN: column == 0}
+
+    def direct(way):
+        return jnp.logical_and(has["gy", way], jnp.logical_not(at_end[way])) if wraps else has["gy", way]
+
+    def wrapped(way):
+        return jnp.logical_and(has["gy", way], at_end[way])
+
+    relays = (
+        jnp.logical_and(column == RUN - 1, gy >= RUN),
+        jnp.logical_and(column == 0, gy + RUN < ny),
+    )
+    peers = [(has["gx", way], neighbour("gx", way)) for way in (UP, DOWN)]
+    peers += [(direct(way), neighbour("gy", way)) for way in (UP, DOWN)]
+    if wraps:
+        ends = jnp.logical_or(at_end[UP], at_end[DOWN])
+        peers += [
+            (jnp.logical_and(ends, gy + RUN < ny), {"gy": gy + RUN}),
+            (jnp.logical_and(ends, gy >= RUN), {"gy": gy - RUN}),
+            (at_end[DOWN], {"gy": gy + (RUN - 1)}),
+            (at_end[UP], {"gy": gy - (RUN - 1)}),
+        ]
 
     loads = {}
 
@@ -69,10 +97,10 @@
     load("mu", mu_in, mu)
 
     barrier = pltpu.get_barrier_semaphore()
-    for (axis, way), there in has.items():
+    for there, device in peers:
         @pl.when(there)
-        def _(axis=axis, way=way):
-            pl.semaphore_signal(barrier, inc=1, device_id=neighbour(axis, way), device_id_type=MESH)
+        def _(device=device):
+            pl.semaphore_signal(barrier, inc=1, device_id=device, device_id_type=MESH)
 
     row = lax.broadcasted_iota(jnp.int32, (cells_y, depth), 0)
     lane = lax.broadcasted_iota(jnp.int32, (cells_y, depth), 1)
@@ -142,9 +170,34 @@
 
     def y_copy(e, way, peer):
         return pltpu.make_async_remote_copy(
-            ys.at[e, way], yr.at[e, way], ys_sem.at[e, way], yr_sem.at[e, way],
+            ys.at[e, way], yr.at[e, way], ys_sem.at[e, way, 0], yr_sem.at[e, way, 0],
             device_id=neighbour("gy", peer), device_id_type=MESH,
         )
+
+    tiles = ys.shape[2] // 2
+
+    def y_hop(e, way, part, step):
+        return pltpu.make_async_remote_copy(
+            ys.at[e, way, pl.ds(part * tiles, tiles)], relayed.at[e, way],
+            ys_sem.at[e, way, part], hop_sem.at[e, way],
+            device_id={"gy": gy + step}, device_id_type=MESH,
+        )
+
+    def y_forward(e, way, part, step):
+        return pltpu.make_async_remote_copy(
+            relayed.at[e, way], yr.at[e, way, pl.ds(part * tiles, tiles)],
+            forward_sem.at[e, way], yr_sem.at[e, way, part],
+            device_id={"gy": gy + step}, device_id_type=MESH,
+        )
+
+    def relay(e):
+        for part, here in enumerate(relays):
+            if wraps:
+                @pl.when(here)
+                def _(part=part):
+                    for way in (UP, DOWN):
+                        y_hop(e, way, part, -TO_RELAY[way, part]).wait_recv()
+                        y_forward(e, way, part, FROM_RELAY[way, part]).start()
 
     odd_block = lax.rem(gx, 2)
     is_near = {UP: odd_block == 0, DOWN: odd_block == 1}
@@ -176,21 +229,46 @@
 
     def send_y(e):
         for way in (UP, DOWN):
-            @pl.when(has["gy", way])
+            @pl.when(direct(way))
             def _(way=way):
                 y_copy(e, way, way).start()
 
+            if wraps:
+                @pl.when(wrapped(way))
+                def _(way=way):
+                    for part in range(2):
+                        y_hop(e, way, part, TO_RELAY[way, part]).start()
+
     def sent_y(e):
         for way in (UP, DOWN):
-            @pl.when(has["gy", way])
+            @pl.when(direct(way))
             def _(way=way):
                 y_copy(e, way, way).wait_send()
 
+            if wraps:
+                @pl.when(wrapped(way))
+                def _(way=way):
+                    for part in range(2):
+                        y_hop(e, way, part, TO_RELAY[way, part]).wait_send()
+
+        for part, here in enumerate(relays):
+            if wraps:
+                @pl.when(here)
+                def _(part=part):
+                    for way in (UP, DOWN):
+                        y_forward(e, way, part, FROM_RELAY[way, part]).wait_send()
+
     def receive_y(e):
         for way in (UP, DOWN):
-            @pl.when(has["gy", 1 - way])
+            @pl.when(direct(1 - way))
             def _(way=way):
                 y_copy(e, way, 1 - way).wait_recv()
+
+            if wraps:
+                @pl.when(wrapped(1 - way))
+                def _(way=way):
+                    for part in range(2):
+                        y_forward(e, way, part, -FROM_RELAY[way, part]).wait_recv()
 
         def unpack(q, odd, p):
             for c in range(3):
@@ -222,7 +300,7 @@
 
     half = pairs // 2
 
-    def stage(e, body, target=None):
+    def stage(e, body, target=None, passing=None):
         receive_y(e)
         receive_x(e, True)
 
@@ -231,6 +309,8 @@
             def _():
                 if target is not None:
                     send_x(target, True)
+                if passing is not None:
+                    relay(passing)
                 receive_x(e, False)
 
             q = lax.rem(i + half * (1 - odd_block), pairs)
@@ -370,7 +450,7 @@
     ready(FS0)
     ready(AS0)
     set_damping()
-    pl.semaphore_wait(barrier, sum(there.astype(jnp.int32) for there in has.values()))
+    pl.semaphore_wait(barrier, sum(there.astype(jnp.int32) for there, _ in peers))
     def send_first(e):
         for near in (False, True):
             send_x(e, near)
@@ -382,17 +462,18 @@
     for name, copy in loads.items():
         if name[0] not in ("px", "py"):
             copy.wait()
+    relay(FS0)
     sent_x(FS0, False)
     send_first(AS0)
 
-    stage(FS0, forward_one, FV1)
-    stage(AS0, adjoint_one, AV1)
-    stage(FV1, forward_stress, FS1)
-    stage(AV1, adjoint_stress, AS1)
-    stage(FS1, forward_two, FV2)
-    stage(AS1, adjoint_two, AV0)
+    stage(FS0, forward_one, FV1, AS0)
+    stage(AS0, adjoint_one, AV1, FV1)
+    stage(FV1, forward_stress, FS1, AV1)
+    stage(AV1, adjoint_stress, AS1, FS1)
+    stage(FS1, forward_two, FV2, AS1)
+    stage(AS1, adjoint_two, AV0, FV2)
     by_plane(density)
-    stage(FV2, image_one)
+    stage(FV2, image_one, None, AV0)
     stage(AV0, image_two)
 
     for e in range(8):
@@ -423,6 +504,7 @@
             pltpu.VMEM((8, 3, cells_x, cells_y + 16, depth), f32),
             pltpu.VMEM(packed, f32),
             pltpu.VMEM(packed, f32),
+            pltpu.VMEM((8, 2, packed[2] // 2, 8, depth), f32),
             pltpu.VMEM((8,) + block, f32),
             pltpu.VMEM((2, 3) + block, f32),
             pltpu.VMEM(block, f32),
@@ -435,6 +517,8 @@
             dma((19,)),
             dma((8, 2, 3)),
             dma((8, 2, 3)),
+            dma((8, 2, 2)),
+            dma((8, 2, 2)),
             dma((8, 2)),
             dma((8, 2)),
         ],

time: 56.5 us -> 62.5 us (1.11)
  the two profiles are of different devices: /device:TPU:393 before, /device:TPU:328 now
where the time goes in v4:
time: 62.5 us; the launch traced here: 62.2 us
  Pallas kernels  57.9 us (93%)
  local copies, waits for them, and re-layouts  3 us (5%)
  between operations  1.3 us (2%)
    pallas_call x1, Pallas kernels, local(): pl.pallas_call(kernel, out_shape=[jax.ShapeDtypeStruct(block, f32)] * 3,...  57.9 us
    unnamed x7, local copies, waits for them, and re-layouts  3 us

profile of v4, /device:TPU:328, one launch (start us, length us, event | category | flops | bytes accessed | tf_op | source)
XLA Modules:
  0.0 62.2 jit_solution(7592318536605448689)
XLA Ops:
  1.3 57.9 %window.1 = (f32[8,16,128]{2,1,0:T(8,128)}, f32[8,16,128]{2,1,0:T(8,128)}, f32[8,16,128]{2,1,0:T(8,128)}) custom-call(f32[9,8,16,128]{3,2,1,0:T(8,128)} %fwd.1, f32[9,8,16,128]{3,2,1,0:T(8,128)} %adj.1, f32[8,16,128]{2,1,0:T(8,128)} %lam_in.1, f32[8,16,128]{2,1,0:T(8,128)} %mu_in.1, f32[8,16,128]{2,1,0:T(8,128)} %buo_in.1, s32[8]{0:T(128)} %src_x.1, ...), custom_call_target="tpu_custom_call" | custom-call | tf_op jit(solution)/shard_map/window/pallas_call | solution.py:497
  59.2 0.0 copy-start.1
  59.2 1.5 %copy.20 = f32[8,16,128]{2,1,0:T(8,128)} copy(f32[8,16,128]{2,1,0:T(8,128)} %get-tuple-element.6) | data formatting | bytes 131072
  60.7 0.0 copy-done.1
  60.8 0.0 copy-start
  60.8 0.6 %copy.21 = f32[8,16,128]{2,1,0:T(8,128)} copy(f32[8,16,128]{2,1,0:T(8,128)S(1)} %copy-done.1) | data formatting | bytes 131072
  61.4 0.2 copy-done
  61.6 0.6 %copy.22 = f32[8,16,128]{2,1,0:T(8,128)} copy(f32[8,16,128]{2,1,0:T(8,128)S(1)} %copy-done) | data formatting | bytes 131072
Async XLA Ops:
  59.2 1.5 %copy-start.1 = (f32[8,16,128]{2,1,0:T(8,128)S(1)}, f32[8,16,128]{2,1,0:T(8,128)}, u32[]{:S(2)}) copy-start(f32[8,16,128]{2,1,0:T(8,128)} %get-tuple-element.7) | copy-start | bytes 196612
  60.8 0.9 %copy-start = (f32[8,16,128]{2,1,0:T(8,128)S(1)}, f32[8,16,128]{2,1,0:T(8,128)}, u32[]{:S(2)}) copy-start(f32[8,16,128]{2,1,0:T(8,128)} %get-tuple-element.8) | copy-start | bytes 196612

commit v5 on v3

--- a/solution.py
+++ b/solution.py
@@ -32,10 +32,11 @@
 
 def kernel(
     fwd, adj, lam_in, mu_in, buo_in, src_x, src_y, src_z, src_w, width_in, rec_x, rec_y, residual,
-    g_lam, g_mu, g_rho,
+    grads,
     px, py, ys, yr, szz, vel0, lam, mu, buo, damp, src, rinj, rates1,
     load_sem, xs_sem, xr_sem, ys_sem, yr_sem,
 ):
+    g_lam, g_mu, g_rho = (grads.at[k] for k in range(3))
     gx, gy = lax.axis_index("gx"), lax.axis_index("gy")
     nx, ny = lax.axis_size("gx"), lax.axis_size("gy")
     cells_x, cells_y, depth = buo.shape
@@ -140,12 +141,6 @@
             device_id=neighbour("gx", peer), device_id_type=MESH,
         )
 
-    def y_copy(e, way, peer):
-        return pltpu.make_async_remote_copy(
-            ys.at[e, way], yr.at[e, way], ys_sem.at[e, way], yr_sem.at[e, way],
-            device_id=neighbour("gy", peer), device_id_type=MESH,
-        )
-
     odd_block = lax.rem(gx, 2)
     is_near = {UP: odd_block == 0, DOWN: odd_block == 1}
 
@@ -174,35 +169,53 @@
                 for c in range(3):
                     x_copy(e, way, c, 1 - way).wait_recv()
 
-    def send_y(e):
+    half = pairs // 2
+    part_of = {True: 1 - odd_block, False: odd_block}
+    tiles = ys.shape[2] // 2
+
+    def y_copy(e, way, near, peer):
+        part = pl.ds(part_of[near] * tiles, tiles)
+        k = 0 if near else 1
+        return pltpu.make_async_remote_copy(
+            ys.at[e, way, part], yr.at[e, way, part], ys_sem.at[e, way, k], yr_sem.at[e, way, k],
+            device_id=neighbour("gy", peer), device_id_type=MESH,
+        )
+
+    def send_y(e, near):
         for way in (UP, DOWN):
             @pl.when(has["gy", way])
             def _(way=way):
-                y_copy(e, way, way).start()
-
-    def sent_y(e):
+                y_copy(e, way, near, way).start()
+
+    def sent_y(e, near):
         for way in (UP, DOWN):
             @pl.when(has["gy", way])
             def _(way=way):
-                y_copy(e, way, way).wait_send()
-
-    def receive_y(e):
+                y_copy(e, way, near, way).wait_send()
+
+    def receive_y(e, near):
         for way in (UP, DOWN):
             @pl.when(has["gy", 1 - way])
             def _(way=way):
-                y_copy(e, way, 1 - way).wait_recv()
-
-        def unpack(q, odd, p):
-            for c in range(3):
-                tile, part = slot(c, q, odd)
-                py[e, c, p, pl.ds(4, 4), :] = yr[e, UP, tile, part, :]
-                py[e, c, p, pl.ds(8 + cells_y, 4), :] = yr[e, DOWN, tile, part, :]
-        by_plane(unpack)
+                y_copy(e, way, near, 1 - way).wait_recv()
+
+        def unpack(i, carry):
+            q = part_of[near] * half + i
+            for odd in range(2):
+                p = 2 * q + odd
+                for c in range(3):
+                    tile, rows4 = slot(c, q, odd)
+                    py[e, c, p, pl.ds(4, 4), :] = yr[e, UP, tile, rows4, :]
+                    py[e, c, p, pl.ds(8 + cells_y, 4), :] = yr[e, DOWN, tile, rows4, :]
+            return carry
+
+        lax.fori_loop(0, half, unpack, 0)
 
     def slot(c, q, odd):
+        start, inside = lax.div(q, half) * tiles, lax.rem(q, half)
         if c < 2:
-            return 2 * q + odd, pl.ds(4 * c, 4)
-        return cells_x + q, pl.ds(4 * odd, 4)
+            return start + 2 * inside + odd, pl.ds(4 * c, 4)
+        return start + 2 * half + inside, pl.ds(4 * odd, 4)
 
     def pack(e, c, q, odd, value):
         tile, part = slot(c, q, odd)
@@ -220,20 +233,20 @@
             return carry
         lax.fori_loop(0, pairs, step, 0)
 
-    half = pairs // 2
-
     def stage(e, body, target=None):
-        receive_y(e)
+        receive_y(e, True)
         receive_x(e, True)
 
         def step(i, carry):
             @pl.when(i == half)
             def _():
                 if target is not None:
+                    send_y(target, True)
                     send_x(target, True)
+                receive_y(e, False)
                 receive_x(e, False)
 
-            q = lax.rem(i + half * (1 - odd_block), pairs)
+            q = lax.rem(i + half * part_of[True], pairs)
             for odd in range(2):
                 body(q, odd, 2 * q + odd)
             return carry
@@ -241,7 +254,7 @@
         lax.fori_loop(0, pairs, step, 0)
         if target is not None:
             send_x(target, False)
-            send_y(target)
+            send_y(target, False)
 
     def diff_x(e, c, p, forward):
         return diff(lambda k: px[e, c, p + (4 + k)], forward)
@@ -372,9 +385,10 @@
     set_damping()
     pl.semaphore_wait(barrier, sum(there.astype(jnp.int32) for there in has.values()))
     def send_first(e):
-        for near in (False, True):
-            send_x(e, near)
-        send_y(e)
+        send_x(e, False)
+        send_y(e, True)
+        send_x(e, True)
+        send_y(e, False)
 
     send_first(FS0)
     set_zeros()
@@ -399,7 +413,8 @@
         if e != FS0:
             sent_x(e, False)
         sent_x(e, True)
-        sent_y(e)
+        sent_y(e, True)
+        sent_y(e, False)
 
 
 def local(
@@ -413,11 +428,11 @@
     hbm, vmem, smem = (pl.BlockSpec(memory_space=m) for m in (pl.ANY, pltpu.VMEM, pltpu.SMEM))
     dma = pltpu.SemaphoreType.DMA
     packed = (8, 2, cells_x + cells_x // 2, 8, depth)
-    return pl.pallas_call(
+    grads = pl.pallas_call(
         kernel,
-        out_shape=[jax.ShapeDtypeStruct(block, f32)] * 3,
+        out_shape=jax.ShapeDtypeStruct((3,) + block, f32),
         in_specs=[hbm] * 5 + [smem] * 5 + [vmem] * 3,
-        out_specs=[vmem] * 3,
+        out_specs=vmem,
         scratch_shapes=[
             pltpu.VMEM((8, 3, cells_x + 8, cells_y, depth), f32),
             pltpu.VMEM((8, 3, cells_x, cells_y + 16, depth), f32),
@@ -435,8 +450,8 @@
             dma((19,)),
             dma((8, 2, 3)),
             dma((8, 2, 3)),
-            dma((8, 2)),
-            dma((8, 2)),
+            dma((8, 2, 2)),
+            dma((8, 2, 2)),
         ],
         compiler_params=pltpu.CompilerParams(
             collective_id=0, has_side_effects=True, vmem_limit_bytes=60 * 1024 * 1024
@@ -447,6 +462,7 @@
         source_x, source_y, source_z, source_wavelet, absorb_width,
         receiver_x.reshape(1, -1), receiver_y.reshape(1, -1), receiver_residual,
     )
+    return grads[0], grads[1], grads[2]
 
 
 def solution(mesh):

time: 56.5 us -> 54.9 us (0.972)
  local copies, waits for them, and re-layouts: 3 us -> 1.58 us
    unnamed x7 -> x0, local copies, waits for them, and re-layouts: 3 us -> none
    squeeze x0 -> x1, local copies, waits for them, and re-layouts: none -> 1.58 us  [local(): return (grads[0], grads[1], grads[2])]
where the time goes in v5:
time: 54.9 us; the launch traced here: 54.7 us
  Pallas kernels  51.8 us (94%)
  local copies, waits for them, and re-layouts  1.58 us (3%)
  between operations  1.29 us (2%)
    pallas_call x1, Pallas kernels, local(): pl.pallas_call(kernel, out_shape=jax.ShapeDtypeStruct((3,) + block, f32),...  51.8 us
    squeeze x1, local copies, waits for them, and re-layouts, local(): return (grads[0], grads[1], grads[2])  1.58 us

profile of v5, /device:TPU:393, one launch (start us, length us, event | category | flops | bytes accessed | tf_op | source)
XLA Modules:
  0.0 54.7 jit_solution(3858971142188517345)
XLA Ops:
  1.3 51.8 %window.1 = f32[3,8,16,128]{3,2,1,0:T(8,128)} custom-call(f32[9,8,16,128]{3,2,1,0:T(8,128)} %fwd.1, f32[9,8,16,128]{3,2,1,0:T(8,128)} %adj.1, f32[8,16,128]{2,1,0:T(8,128)} %lam_in.1, f32[8,16,128]{2,1,0:T(8,128)} %mu_in.1, f32[8,16,128]{2,1,0:T(8,128)} %buo_in.1, s32[8]{0:T(128)} %src_x.1, s32[8]{0:T(128)} %src_y.1, s32[8]{0:T(128)} %src_z.1, f32[8]{0:T(128)} %src_w.1, ...), custom_call_target="tpu_custom_call" | custom-call | tf_op jit(solution)/shard_map/window/pallas_call | solution.py:431
  53.1 1.6 %slice_bitcast_fusion = (f32[8,16,128]{2,1,0:T(8,128)}, f32[8,16,128]{2,1,0:T(8,128)}, f32[8,16,128]{2,1,0:T(8,128)}) fusion(f32[3,8,16,128]{3,2,1,0:T(8,128)} %window.1), kind=kLoop, calls=%fused_computation | loop fusion | bytes 393216 | tf_op jit(solution)/shard_map/squeeze | solution.py:465

commit v6 on v5

--- a/solution.py
+++ b/solution.py
@@ -49,6 +49,12 @@
     def neighbour(axis, way):
         return {axis: place[axis] + (1 if way == UP else -1)}
 
+    barrier = pltpu.get_barrier_semaphore()
+    for (axis, way), there in has.items():
+        @pl.when(there)
+        def _(axis=axis, way=way):
+            pl.semaphore_signal(barrier, inc=1, device_id=neighbour(axis, way), device_id_type=MESH)
+
     loads = {}
 
     def load(name, source, target):
@@ -68,12 +74,6 @@
     load("buo", buo_in, buo)
     load("lam", lam_in, lam)
     load("mu", mu_in, mu)
-
-    barrier = pltpu.get_barrier_semaphore()
-    for (axis, way), there in has.items():
-        @pl.when(there)
-        def _(axis=axis, way=way):
-            pl.semaphore_signal(barrier, inc=1, device_id=neighbour(axis, way), device_id_type=MESH)
 
     row = lax.broadcasted_iota(jnp.int32, (cells_y, depth), 0)
     lane = lax.broadcasted_iota(jnp.int32, (cells_y, depth), 1)
@@ -369,7 +369,7 @@
     forward_two = velocity_half(FS1, FV2, lambda c, p: center_x(FV1, c, p))
     adjoint_two = velocity_half(AS1, AV0, lambda c, p: adjoint_velocity(AV1, 0, c, p))
 
-    def ready(e):
+    def send_first_y(e):
         for c in range(3):
             loads["py", e, c].wait()
 
@@ -377,27 +377,25 @@
             for c in range(3):
                 pack(e, c, q, odd, center_y(e, c, p))
         by_plane(first)
-        for c in range(3):
-            loads["px", e, c].wait()
-
-    ready(FS0)
-    ready(AS0)
+        send_y(e, True)
+        send_y(e, False)
+
+    for c in range(3):
+        loads["px", FS0, c].wait()
+    pl.semaphore_wait(barrier, sum(there.astype(jnp.int32) for there in has.values()))
+    send_x(FS0, False)
+    send_x(FS0, True)
+    send_first_y(FS0)
     set_damping()
-    pl.semaphore_wait(barrier, sum(there.astype(jnp.int32) for there in has.values()))
-    def send_first(e):
-        send_x(e, False)
-        send_y(e, True)
-        send_x(e, True)
-        send_y(e, False)
-
-    send_first(FS0)
     set_zeros()
     set_injections()
     for name, copy in loads.items():
-        if name[0] not in ("px", "py"):
+        if name[0] not in ("px", "py") or name[:2] == ("px", AS0):
             copy.wait()
     sent_x(FS0, False)
-    send_first(AS0)
+    send_x(AS0, False)
+    send_x(AS0, True)
+    send_first_y(AS0)
 
     stage(FS0, forward_one, FV1)
     stage(AS0, adjoint_one, AV1)

time: 54.9 us -> 54.9 us (level)
  no operation moved by 1% of the time
where the time goes in v6:
time: 54.9 us; the launch traced here: 54.7 us
  Pallas kernels  51.8 us (94%)
  local copies, waits for them, and re-layouts  1.58 us (3%)
  between operations  1.29 us (2%)
    pallas_call x1, Pallas kernels, local(): pl.pallas_call(kernel, out_shape=jax.ShapeDtypeStruct((3,) + block, f32),...  51.8 us
    squeeze x1, local copies, waits for them, and re-layouts, local(): return (grads[0], grads[1], grads[2])  1.58 us

profile of v6, /device:TPU:393, one launch (start us, length us, event | category | flops | bytes accessed | tf_op | source)
XLA Modules:
  0.0 54.7 jit_solution(9462988748220192738)
XLA Ops:
  1.3 51.8 %window.1 = f32[3,8,16,128]{3,2,1,0:T(8,128)} custom-call(f32[9,8,16,128]{3,2,1,0:T(8,128)} %fwd.1, f32[9,8,16,128]{3,2,1,0:T(8,128)} %adj.1, f32[8,16,128]{2,1,0:T(8,128)} %lam_in.1, f32[8,16,128]{2,1,0:T(8,128)} %mu_in.1, f32[8,16,128]{2,1,0:T(8,128)} %buo_in.1, s32[8]{0:T(128)} %src_x.1, s32[8]{0:T(128)} %src_y.1, s32[8]{0:T(128)} %src_z.1, f32[8]{0:T(128)} %src_w.1, ...), custom_call_target="tpu_custom_call" | custom-call | tf_op jit(solution)/shard_map/window/pallas_call | solution.py:429
  53.1 1.6 %slice_bitcast_fusion = (f32[8,16,128]{2,1,0:T(8,128)}, f32[8,16,128]{2,1,0:T(8,128)}, f32[8,16,128]{2,1,0:T(8,128)}) fusion(f32[3,8,16,128]{3,2,1,0:T(8,128)} %window.1), kind=kLoop, calls=%fused_computation | loop fusion | bytes 393216 | tf_op jit(solution)/shard_map/squeeze | solution.py:463

commit v7 on v5

--- a/solution.py
+++ b/solution.py
@@ -391,13 +391,12 @@
         send_y(e, False)
 
     send_first(FS0)
+    send_first(AS0)
     set_zeros()
     set_injections()
     for name, copy in loads.items():
         if name[0] not in ("px", "py"):
             copy.wait()
-    sent_x(FS0, False)
-    send_first(AS0)
 
     stage(FS0, forward_one, FV1)
     stage(AS0, adjoint_one, AV1)
@@ -410,8 +409,7 @@
     stage(AV0, image_two)
 
     for e in range(8):
-        if e != FS0:
-            sent_x(e, False)
+        sent_x(e, False)
         sent_x(e, True)
         sent_y(e, True)
         sent_y(e, False)

time: 54.9 us -> 54.9 us (level)
  no operation moved by 1% of the time
where the time goes in v7:
time: 54.9 us; the launch traced here: 54.7 us
  Pallas kernels  51.8 us (94%)
  local copies, waits for them, and re-layouts  1.58 us (3%)
  between operations  1.29 us (2%)
    pallas_call x1, Pallas kernels, local(): pl.pallas_call(kernel, out_shape=jax.ShapeDtypeStruct((3,) + block, f32),...  51.8 us
    squeeze x1, local copies, waits for them, and re-layouts, local(): return (grads[0], grads[1], grads[2])  1.58 us

profile of v7, /device:TPU:393, one launch (start us, length us, event | category | flops | bytes accessed | tf_op | source)
XLA Modules:
  0.0 54.7 jit_solution(2874631157024381024)
XLA Ops:
  1.3 51.8 %window.1 = f32[3,8,16,128]{3,2,1,0:T(8,128)} custom-call(f32[9,8,16,128]{3,2,1,0:T(8,128)} %fwd.1, f32[9,8,16,128]{3,2,1,0:T(8,128)} %adj.1, f32[8,16,128]{2,1,0:T(8,128)} %lam_in.1, f32[8,16,128]{2,1,0:T(8,128)} %mu_in.1, f32[8,16,128]{2,1,0:T(8,128)} %buo_in.1, s32[8]{0:T(128)} %src_x.1, s32[8]{0:T(128)} %src_y.1, s32[8]{0:T(128)} %src_z.1, f32[8]{0:T(128)} %src_w.1, ...), custom_call_target="tpu_custom_call" | custom-call | tf_op jit(solution)/shard_map/window/pallas_call | solution.py:429
  53.1 1.6 %slice_bitcast_fusion = (f32[8,16,128]{2,1,0:T(8,128)}, f32[8,16,128]{2,1,0:T(8,128)}, f32[8,16,128]{2,1,0:T(8,128)}) fusion(f32[3,8,16,128]{3,2,1,0:T(8,128)} %window.1), kind=kLoop, calls=%fused_computation | loop fusion | bytes 393216 | tf_op jit(solution)/shard_map/squeeze | solution.py:463
